TPU v7x, 256 devices: a whole 4x4x8 slice. The times are simulated.
256 devices in a mesh: dom: 32 (over y, z), rep: 8 (over x, core).
Axes of the slice: x: 4, y: 4, z: 8, core: 2. Of those that a mesh axis runs over, the one named last changes fastest.
Arguments:
- queries: bfloat16 [16384, 256], P(('dom', 'rep')), may hold values from -80 to 80
- probes: int32 [16384, 8], P(('dom', 'rep')), may hold values from 0 to 63, all different within a row; in each aligned block of 64 rows (0 to 63, 64 to 127, ...) at most 16 rows name the same one
- corpus: bfloat16 [64, 8192, 256], P('dom', 'rep'), may hold values from -20 to 20
- labels: int32 [64, 8192], P('dom', 'rep'), may hold values from 0 to 127
Outputs:
- type_scores: float32 [16384, 128], P(('dom', 'rep'))
Inputs may be any that keep to these rules, and one draw needn't show every extreme that they name: `probes`: each query names 8 different partitions. The 64 queries of one device name one partition at most 16 times, a bound that some block reaches.
All inputs are finite; a program needn't handle non-finite values.
Results may differ from a plain program's by a relative error of at most 0.00085.
Values may be sent and summed in bfloat16 or wider, within the bound.
A program may use at most 128 MiB of HBM per device.

v0:
```python
import math

import jax
import jax.numpy as jnp
from jax import lax
from jax.sharding import PartitionSpec as P

NCLASS = 128


def pair_ranks(probe_rows, num_parts):
    matches = (
        probe_rows[:, :, None] == jnp.arange(num_parts, dtype=jnp.int32)[None, None, :]
    ).astype(jnp.int32)
    earlier = jnp.cumsum(matches, axis=1) - matches
    return jnp.sum(earlier * matches, axis=-1)


def local(queries, probes, corpus, labels):
    num_rep = lax.axis_size("rep")
    num_dom = lax.axis_size("dom")
    my_rep = lax.axis_index("rep")
    local_parts = corpus.shape[0]
    feature_dim = queries.shape[1]
    per_device = queries.shape[0]
    num_probes = probes.shape[1]
    num_parts = local_parts * num_dom
    capacity = 2 * per_device * num_probes // num_parts
    own_ranks = pair_ranks(probes.reshape(1, -1), num_parts)[0]
    flat_parts = probes.reshape(-1)
    every_query, every_probe = (
        lax.all_gather(queries, "rep", axis=0, tiled=True),
        lax.all_gather(probes, "rep", axis=0, tiled=True),
    )
    wide_ranks = pair_ranks(every_probe.reshape(num_rep, per_device * num_probes), num_parts)
    wide_slots = (jnp.arange(num_rep, dtype=jnp.int32)[:, None] * capacity + wide_ranks).reshape(-1)
    wide_rows = jnp.arange(num_rep * per_device * num_probes, dtype=jnp.int32) // num_probes
    outbox = jnp.zeros((num_parts, num_rep * capacity, feature_dim), jnp.bfloat16)
    outbox = outbox.at[every_probe.reshape(-1), wide_slots].set(every_query[wide_rows])
    arrived = lax.all_to_all(outbox, "dom", split_axis=0, concat_axis=1, tiled=True)
    total_slots = arrived.shape[1]
    own_slots = total_slots // num_rep
    block_rows = math.gcd(total_slots, 512)
    score_scale = feature_dim ** (-0.5)
    class_ids = jnp.arange(NCLASS, dtype=jnp.int32)
    peak_list = []
    for part_index in range(local_parts):
        stripe_keys = corpus[part_index]

        def score_of(query_block):
            return (
                jnp.einsum(
                    "qd,rd->qr", query_block, stripe_keys, preferred_element_type=jnp.float32
                )
                * score_scale
            )

        def peak_of(query_block):
            return jnp.max(score_of(query_block), axis=1)

        blocks = arrived[part_index].reshape(-1, block_rows, feature_dim)
        block_peaks = lax.map(peak_of, blocks)
        peak_list.append(block_peaks.reshape(-1))
    peaks = lax.pmax(jnp.stack(peak_list), "rep")
    class_list = []
    total_list = []
    for part_index in range(local_parts):
        stripe_keys = corpus[part_index]
        one_hot = (labels[part_index][:, None] == class_ids[None, :]).astype(jnp.float32)

        def finish(scores, peak_block):
            weights = jnp.exp(scores - peak_block[:, None])
            totals = jnp.sum(weights, axis=1)
            class_sums = jnp.dot(weights, one_hot, precision=lax.Precision.HIGHEST)
            return (class_sums, totals)

        def weigh_block(inputs):
            query_block, peak_block = inputs
            scores = (
                jnp.einsum(
                    "qd,rd->qr", query_block, stripe_keys, preferred_element_type=jnp.float32
                )
                * score_scale
            )
            return finish(scores, peak_block)

        peak_blocks = peaks[part_index].reshape(-1, block_rows)
        blocks = arrived[part_index].reshape(-1, block_rows, feature_dim)
        class_sums, totals = lax.map(weigh_block, (blocks, peak_blocks))
        class_list.append(class_sums.reshape(total_slots, NCLASS))
        total_list.append(totals.reshape(total_slots))
    class_parts = jnp.stack(class_list)
    total_parts = jnp.stack(total_list)

    def rep_major(tensor):
        shape = tensor.shape
        grouped = tensor.reshape((local_parts, num_dom, num_rep, capacity) + shape[2:])
        return jnp.swapaxes(grouped, 1, 2).reshape(shape)

    class_parts = rep_major(class_parts)
    total_parts = rep_major(total_parts)
    peaks = rep_major(peaks)
    summed_classes, summed_totals = (
        lax.psum_scatter(class_parts, "rep", scatter_dimension=1, tiled=True),
        lax.psum_scatter(total_parts, "rep", scatter_dimension=1, tiled=True),
    )
    own_peaks = lax.dynamic_slice_in_dim(peaks, my_rep * own_slots, own_slots, 1)
    back_classes, back_totals, back_peaks = (
        lax.all_to_all(summed_classes, "dom", split_axis=1, concat_axis=0, tiled=True),
        lax.all_to_all(summed_totals, "dom", split_axis=1, concat_axis=0, tiled=True),
        lax.all_to_all(own_peaks, "dom", split_axis=1, concat_axis=0, tiled=True),
    )
    pair_peaks = back_peaks[flat_parts, own_ranks].reshape(per_device, num_probes)
    pair_totals = back_totals[flat_parts, own_ranks].reshape(per_device, num_probes)
    pair_classes = back_classes[flat_parts, own_ranks].reshape(per_device, num_probes, NCLASS)
    top_peak = jnp.max(pair_peaks, axis=1, keepdims=True)
    factors = jnp.exp(pair_peaks - top_peak)
    numerator = jnp.sum(factors[:, :, None] * pair_classes, axis=1)
    denominator = jnp.sum(factors * pair_totals, axis=1)
    return NCLASS * numerator / denominator[:, None]


def solution(mesh):
    in_specs = (
        P(("dom", "rep"), None),
        P(("dom", "rep"), None),
        P("dom", "rep", None),
        P("dom", "rep"),
    )
    out_specs = P(("dom", "rep"), None)
    return jax.shard_map(local, mesh=mesh, in_specs=in_specs, out_specs=out_specs, check_vma=False)
```

profile of v0, /device:TPU:1, one launch (start us, length us, event | category | flops | bytes accessed | tf_op | source)
XLA Modules:
  0.0 404.2 jit_solution(4092328308725640562)
XLA Ops:
  6.5 16.0 %all-gather = s32[8,64,8]{1,2,0:T(8,128)S(1)} all-gather(s32[1,64,8]{1,2,0:T(8,128)} %bitcast.194), channel_id=1, replica_groups=mesh['dom'=32,'rep'=8] {'rep'}, dimensions={0}, use_global_device_ids=true | all-gather | bytes 18432 | tf_op jit(solution)/shard_map/all_gather | solution.py:33
  23.3 9.5 %reduce-window.14 = s32[8,64,4,128]{3,1,2,0:T(8,128)S(1)} reduce-window(s32[8,64,4,128]{3,1,2,0:T(8,128)S(1)} %fusion.42, s32[]{:T(128)} %constant.93.clone.1), window={size=1x1x1x128 pad=0_0x0_0x0_0x127_0}, to_apply=%region_0.0 | reduce-window | flops 33292288 | bytes 2097156 | tf_op jit(solution)/shard_map/reduce-window
  34.6 12.9 %all_gather.7 = bf16[512,256]{1,0:T(8,128)(2,1)S(1)} all-gather(bf16[64,256]{1,0:T(8,128)(2,1)S(1)} %copy-done.5), channel_id=1, replica_groups=mesh['dom'=32,'rep'=8] {'rep'}, dimensions={0}, use_global_device_ids=true | all-gather | bytes 294912 | tf_op jit(solution)/shard_map/all_gather | solution.py:32
  47.5 33.4 %scatter_custom_fusion = bf16[8192,256]{1,0:T(8,128)(2,1)} fusion(s32[4096]{0:T(1024)S(1)} %broadcast_select_fusion, bf16[512,256]{1,0:T(8,128)(2,1)S(1)} %all_gather.7, s32[4096]{0:T(1024)S(1)} %broadcast_clamp_fusion, bf16[]{:T(256)} %constant.95.clone.1), kind=kCustom, calls=%fused_computation.48 | custom fusion | bytes 4194306
  80.9 10.1 %all-to-all-start = ((bf16[64,128,256]{2,1,0:T(8,128)(2,1)}), bf16[64,128,256]{2,1,0:T(8,128)(2,1)}, u32[]{:S(2)}, u32[]{:S(2)}) async-start(bf16[64,128,256]{2,1,0:T(8,128)(2,1)} %bitcast.165), calls=%async_computation | async-start | bytes 8388608 | tf_op jit(solution)/shard_map/all_to_all | solution.py:40
  91.1 94.1 %all-to-all-done = bf16[64,128,256]{2,1,0:T(8,128)(2,1)} async-done(((bf16[64,128,256]{2,1,0:T(8,128)(2,1)}), bf16[64,128,256]{2,1,0:T(8,128)(2,1)}, u32[]{:S(2)}, u32[]{:S(2)}) %all-to-all-start) | async-done | bytes 4194336 | tf_op jit(solution)/shard_map/all_to_all | solution.py:40
  185.2 3.9 fusion.52
  189.2 12.6 %while.46 = (s32[]{:T(128)}, f32[8,512]{1,0:T(8,128)S(1)}, bf16[8,512,256]{2,1,0:T(8,128)(2,1)}, bf16[1024,256]{1,0:T(8,128)(2,1)S(1)}, s32[]{:T(128)}, /*index=5*/s32[]{:T(128)}) while((s32[]{:T(128)}, f32[8,512]{1,0:T(8,128)S(1)}, bf16[8,512,256]{2,1,0:T(8,128)(2,1)}, bf16[1024,256]{1,0:T(8,128)(2,1)S(1)}, s32[]{:T(128)}, ...), condition=%wide.region_6.7_spmd, body=%wide.region_4.6_spmd.sunk | while | flops 269483520 | bytes 793161 | solution.py:62
  201.9 5.1 %while.47 = (s32[]{:T(128)}, f32[8,512]{1,0:T(8,128)S(1)}, bf16[8,512,256]{2,1,0:T(8,128)(2,1)S(1)}, bf16[1024,256]{1,0:T(8,128)(2,1)S(1)}, s32[]{:T(128)}, /*index=5*/s32[]{:T(128)}) while((s32[]{:T(128)}, f32[8,512]{1,0:T(8,128)S(1)}, bf16[8,512,256]{2,1,0:T(8,128)(2,1)S(1)}, bf16[1024,256]{1,0:T(8,128)(2,1)S(1)}, s32[]{:T(128)}, ...), condition=%wide.region_9.10_spmd, body=%wide.region_7.9_spmd.sunk | while | flops 269483520 | bytes 792653 | solution.py:62
  207.0 22.4 %pmax.7 = f32[2,4096]{1,0:T(2,128)S(1)} all-reduce(f32[2,4096]{1,0:T(2,128)S(1)} %pad_maximum_fusion), channel_id=1, replica_groups=mesh['dom'=32,'rep'=8] {'rep'}, use_global_device_ids=true, to_apply=%region_10.11 | all-reduce | flops 8192 | bytes 65536 | tf_op jit(solution)/shard_map/pmax | solution.py:64
  230.0 29.7 %while.48 = (s32[]{:T(128)}, f32[8,512,128]{2,1,0:T(8,128)S(1)}, f32[8,512]{1,0:T(8,128)S(1)}, bf16[8,512,256]{2,1,0:T(8,128)(2,1)}, bf16[1024,256]{1,0:T(8,128)...) while((s32[]{:T(128)}, f32[8,512,128]{2,1,0:T(8,128)S(1)}, ...), condition=%wide.region_17.18_spmd.clone, body=%wide.region_15.17_spmd.clone.sunk | while | flops 1076624896 | bytes 5261929 | solution.py:89
  231.6 2.0 fusion.77
  235.4 2.0 fusion.77
  239.1 2.0 fusion.77
  242.8 2.0 fusion.77
  246.5 2.0 fusion.77
  250.3 2.0 fusion.77
  254.0 2.0 fusion.77
  257.7 2.0 fusion.77
  261.2 29.8 %while.49 = (s32[]{:T(128)}, f32[8,512,128]{2,1,0:T(8,128)S(1)}, f32[8,512]{1,0:T(8,128)S(1)}, bf16[8,512,256]{2,1,0:T(8,128)(2,1)}, bf16[1024,256]{1,0:T(8,128)...) while((s32[]{:T(128)}, f32[8,512,128]{2,1,0:T(8,128)S(1)}, ...), condition=%wide.region_20.21_spmd.clone, body=%wide.region_18.20_spmd.clone.sunk | while | flops 1076624896 | bytes 5261929 | solution.py:89
  261.3 1.6 fusion.80
  262.9 2.0 fusion.81
  265.0 1.6 fusion.80
  266.6 2.0 fusion.81
  268.7 1.6 fusion.80
  270.3 2.0 fusion.81
  272.4 1.6 fusion.80
  274.0 2.0 fusion.81
  276.2 1.6 fusion.80
  277.8 2.0 fusion.81
  279.9 1.6 fusion.80
  281.5 2.0 fusion.81
  283.6 1.6 fusion.80
  285.2 2.0 fusion.81
  288.9 2.0 fusion.81
  291.2 2.9 copy.59
  294.1 2.0 maximum_bitcast_fusion
  296.1 2.4 copy.51
  300.3 7.7 %all-to-all-start.1 = ((f32[2,32,16]{2,0,1:T(2,128)}), f32[2,32,16]{2,0,1:T(2,128)S(1)}, u32[]{:S(2)}, u32[]{:S(2)}) async-start(f32[2,32,16]{2,0,1:T(2,128)} %copy.45), calls=%async_computation.1 | async-start | bytes 65536 | tf_op jit(solution)/shard_map/all_to_all | solution.py:111
  308.1 19.8 %reduce-scatter.7.cloned.1.call-done = f32[512,2]{1,0:T(8,128)} async-done(((f32[4096,2]{1,0:T(8,128)}), f32[512,2]{1,0:T(8,128)}) %reduce-scatter.7.cloned.1.call-update) | async-done | bytes 4112
  327.9 1.8 copy.56
  329.7 9.2 %all-to-all-start.3 = ((f32[2,32,16]{2,0,1:T(2,128)}), f32[2,32,16]{2,0,1:T(2,128)S(1)}, u32[]{:S(2)}, u32[]{:S(2)}) async-start(f32[2,32,16]{2,0,1:T(2,128)} %copy.56), calls=%async_computation.4 | async-start | bytes 65536 | tf_op jit(solution)/shard_map/all_to_all | solution.py:110
  339.1 30.5 %reduce-scatter.5.cloned.1.call-done = f32[2,512,128]{2,1,0:T(8,128)} async-done(((f32[2,4096,128]{2,1,0:T(8,128)}), f32[2,512,128]{2,1,0:T(8,128)}) %reduce-scatter.5.cloned.1.call-update) | async-done | bytes 524304 | tf_op jit(solution)/shard_map/reduce_scatter | solution.py:104
  369.7 2.2 copy.52
  371.9 9.4 %all-to-all-start.2 = ((f32[2,512,128]{2,0,1:T(2,128)}), f32[2,512,128]{2,0,1:T(2,128)S(1)}, u32[]{:S(2)}, u32[]{:S(2)}) async-start(f32[2,512,128]{2,0,1:T(2,128)} %copy.52), calls=%async_computation.3 | async-start | bytes 1048576 | tf_op jit(solution)/shard_map/all_to_all | solution.py:109
  383.6 3.8 gather_fusion
  387.6 3.8 gather_fusion.2
  392.8 3.7 gather_fusion.1
  (165 shorter events, 44.3 us)
Async XLA Ops:
  32.8 1.5 copy-start.9
  32.8 1.6 copy-start.8
  32.8 1.7 copy-start.5
  80.8 10.1 %copy-start.7 = (s32[2,1024]{1,0:T(2,128)S(1)}, s32[2,1024]{1,0:T(2,128)}, u32[]{:S(2)}) copy-start(s32[2,1024]{1,0:T(2,128)} %param.15) | copy-start | bytes 24580
  80.8 10.2 %copy-start.2 = (bf16[2,1024,256]{2,1,0:T(8,128)(2,1)S(1)}, bf16[2,1024,256]{2,1,0:T(8,128)(2,1)}, u32[]{:S(2)}) copy-start(bf16[2,1024,256]{2,1,0:T(8,128)(2,1)} %param.14) | copy-start | bytes 3145732
  80.9 104.4 %all-to-all-start = ((bf16[64,128,256]{2,1,0:T(8,128)(2,1)}), bf16[64,128,256]{2,1,0:T(8,128)(2,1)}, u32[]{:S(2)}, u32[]{:S(2)}) async-start(bf16[64,128,256]{2,1,0:T(8,128)(2,1)} %bitcast.165), calls=%async_computation | async-start | bytes 8388608 | tf_op jit(solution)/shard_map/all_to_all | solution.py:40
  90.9 237.0 %reduce-scatter.7.cloned.1.call-start = ((), (), s32[]{:S(2)}) async-start(), calls=%async_computation.7 | async-start | bytes 2359296
  206.9 22.6 %copy-start.1 = (bf16[8,512,256]{2,1,0:T(8,128)(2,1)}, bf16[8,512,256]{2,1,0:T(8,128)(2,1)S(1)}, u32[]{:S(2)}) copy-start(bf16[8,512,256]{2,1,0:T(8,128)(2,1)S(1)} %get-tuple-element.470) | copy-start | bytes 6291460
  229.4 0.6 copy-start.3
  259.8 1.3 copy-start
  294.1 75.6 %reduce-scatter.5.cloned.1.call-start = ((), (), s32[]{:S(2)}) async-start(), calls=%async_computation.6 | async-start | bytes 4718592 | tf_op jit(solution)/shard_map/reduce_scatter | solution.py:104
  298.5 0.8 copy-start.4
  298.5 40.5 %copy-start.6 = (s32[64,8]{0,1:T(8,128)S(1)}, s32[64,8]{0,1:T(8,128)}, u32[]{:S(2)}) copy-start(s32[64,8]{0,1:T(8,128)} %param.13) | copy-start | bytes 6148
  300.3 29.4 %all-to-all-start.1 = ((f32[2,32,16]{2,0,1:T(2,128)}), f32[2,32,16]{2,0,1:T(2,128)S(1)}, u32[]{:S(2)}, u32[]{:S(2)}) async-start(f32[2,32,16]{2,0,1:T(2,128)} %copy.45), calls=%async_computation.1 | async-start | bytes 65536 | tf_op jit(solution)/shard_map/all_to_all | solution.py:111
  329.7 42.1 %all-to-all-start.3 = ((f32[2,32,16]{2,0,1:T(2,128)}), f32[2,32,16]{2,0,1:T(2,128)S(1)}, u32[]{:S(2)}, u32[]{:S(2)}) async-start(f32[2,32,16]{2,0,1:T(2,128)} %copy.56), calls=%async_computation.4 | async-start | bytes 65536 | tf_op jit(solution)/shard_map/all_to_all | solution.py:110
  371.9 20.9 %all-to-all-start.2 = ((f32[2,512,128]{2,0,1:T(2,128)}), f32[2,512,128]{2,0,1:T(2,128)S(1)}, u32[]{:S(2)}, u32[]{:S(2)}) async-start(f32[2,512,128]{2,0,1:T(2,128)} %copy.52), calls=%async_computation.3 | async-start | bytes 1048576 | tf_op jit(solution)/shard_map/all_to_all | solution.py:109
Sparse Core Ops, SparseCore 0:
  294.2 33.6 reduce-scatter.6
  330.5 39.1 reduce-scatter.4
where the time goes:
time: 412 us; the launch traced here: 404 us
  waiting for transfers between devices  146 us (35%)
  matrix products  74.3 us (18%)
  local copies, waits for them, and re-layouts  66.3 us (16%)
  blocking collectives  51.3 us (12%)
  starting transfers between devices  36.5 us (9%)
  other arithmetic  15.4 us (4%)
  between operations  13.9 us (3%)
    all_to_all x1, waiting for transfers between devices, local(): lax.all_to_all(outbox, 'dom', split_axis=0, concat_axis=1, tiled=True)  94.1 us
    unnamed x26, local copies, waits for them, and re-layouts  38.7 us
    dot_general x16, matrix products, finish(): class_sums = jnp.dot(weights, one_hot, precision=lax.Precision.HIGHEST)  32.3 us
    reduce_scatter x1, waiting for transfers between devices, local(): lax.psum_scatter(class_parts, 'rep', scatter_dimension=1, tiled=True)  30.5 us
    dot_general x16, matrix products, weigh_block(): jnp.einsum('qd,rd->qr', query_block, stripe_keys, preferred_element_type=...  25.6 us
    pmax x1, blocking collectives, local(): peaks = lax.pmax(jnp.stack(peak_list), 'rep')  22.4 us
    unnamed x3, waiting for transfers between devices  19.9 us
    dot_general x16, matrix products, score_of(): jnp.einsum('qd,rd->qr', query_block, stripe_keys, preferred_element_type=...  16.4 us
  transfers between devices with their start and end apart: 6, of which 4 were waited for; matrix products, arithmetic and copies ran while one was open for 5% of the time, Pallas kernels for 0%

commit v1 on v0

v1 whole, which is shorter than its diff:
```python
import functools
import math

import jax
import jax.numpy as jnp
from jax import lax
from jax.experimental import pallas as pl
from jax.experimental.pallas import tpu as pltpu
from jax.sharding import PartitionSpec as P

NCLASS = 128
CAP = 16
PARTS = 2
MESH = pl.DeviceIdType.MESH
NT = (((1,), (1,)), ((), ()))


def select_mask(probes_ref, nd):
    nq, npr = probes_ref.shape
    nparts = PARTS * nd
    width = max(128, nparts)
    part_ids = lax.broadcasted_iota(jnp.int32, (nq, width), 1)
    match = jnp.zeros((nq, width), jnp.float32)
    for j in range(npr):
        match = jnp.where(probes_ref[:, j : j + 1] == part_ids, 1.0, match)
    row = lax.broadcasted_iota(jnp.int32, (nq, nq), 0)
    col = lax.broadcasted_iota(jnp.int32, (nq, nq), 1)
    earlier = jnp.where(col < row, 1.0, 0.0).astype(jnp.bfloat16)
    rank = jnp.dot(earlier, match.astype(jnp.bfloat16), preferred_element_type=jnp.float32)
    code = jnp.where(match > 0.0, rank, -1.0)
    slots = nparts * CAP
    part_row = lax.broadcasted_iota(jnp.int32, (width, slots), 0)
    lane = lax.broadcasted_iota(jnp.int32, (width, slots), 1)
    half = nd * CAP
    lane_part = PARTS * ((lane % half) // CAP) + lane // half
    spread = jnp.where(part_row == lane_part, 1.0, 0.0).astype(jnp.bfloat16)
    wide = jnp.dot(code.astype(jnp.bfloat16), spread, preferred_element_type=jnp.float32)
    slot = (lax.broadcasted_iota(jnp.int32, (nq, slots), 1) % CAP).astype(jnp.float32)
    return jnp.where(wide == slot, 1.0, 0.0)


def kernel(
    nd, nx,
    q_ref, probes_ref, corpus_ref, labels_ref, out_ref,
    mask, outbox, inbox, kbuf, lab, acc, m_s, mout, pin, ret,
    ks, kr, qs, qr, ls, lr, rs, rr, ps, pr,
):
    dom = lax.axis_index("dom")
    rep = lax.axis_index("rep")
    nrep = 2 * nx
    x, c = rep // 2, rep % 2
    rows = corpus_ref.shape[1]
    hr = rows // 2
    half = nd * CAP
    right = (dom, ((x + 1) % nx) * 2 + c)
    left = (dom, ((x + nx - 1) % nx) * 2 + c)
    sibling = (dom, x * 2 + (1 - c))

    barrier = pltpu.get_barrier_semaphore()

    def greet_dom(k, carry):
        pl.semaphore_signal(barrier, inc=1, device_id=((dom + k) % nd, rep), device_id_type=MESH)
        return carry

    def greet_rep(k, carry):
        pl.semaphore_signal(barrier, inc=1, device_id=(dom, (rep + k) % nrep), device_id_type=MESH)
        return carry

    lax.fori_loop(1, nd, greet_dom, 0)
    lax.fori_loop(1, nrep, greet_rep, 0)

    def own_copy(p, h):
        return pltpu.make_async_copy(
            corpus_ref.at[p, pl.ds(h * hr, hr)], kbuf.at[p, rep, pl.ds(h * hr, hr)], kr.at[p, rep, h]
        )

    for p in range(PARTS):
        for h in range(2):
            own_copy(p, h).start()
    own_lab = pltpu.make_async_copy(labels_ref, lab.at[rep], lr)
    own_lab.start()

    sel = select_mask(probes_ref, nd)
    mask[...] = sel
    picked = lax.dot_general(
        sel.T.astype(jnp.bfloat16), q_ref[...], (((1,), (0,)), ((), ())), preferred_element_type=jnp.float32
    )
    outbox[...] = picked.astype(jnp.bfloat16).reshape(outbox.shape)

    pl.semaphore_wait(barrier, nd - 1 + nrep - 1)

    def send(p, chunk, h, device, k):
        rows_h = pl.ds(h * hr, hr)
        return pltpu.make_async_remote_copy(
            src_ref=kbuf.at[p, chunk, rows_h],
            dst_ref=kbuf.at[p, chunk, rows_h],
            send_sem=ks.at[p, k],
            recv_sem=kr.at[p, chunk, h],
            device_id=device,
            device_id_type=MESH,
        )

    def chunk_at(dx, col):
        return ((x + dx) % nx) * 2 + col

    cl, cr, co = chunk_at(nx - 1, c), chunk_at(1, c), chunk_at(2, c)

    def moves(p):
        return {
            "r0": (p, rep, 0, right, 0),
            "r1": (p, rep, 1, right, 1),
            "l1": (p, rep, 1, left, 2),
            "l0": (p, rep, 0, left, 3),
            "rr": (p, cl, 0, right, 4),
            "ll": (p, cr, 1, left, 5),
            "s0": (p, rep, 0, sibling, 6),
            "s1": (p, rep, 1, sibling, 7),
            "sl0": (p, cl, 0, sibling, 8),
            "sl1": (p, cl, 1, sibling, 9),
            "sr0": (p, cr, 0, sibling, 10),
            "sr1": (p, cr, 1, sibling, 11),
            "so0": (p, co, 0, sibling, 12),
            "so1": (p, co, 1, sibling, 13),
        }

    def start(p, *names):
        table = moves(p)
        for name in names:
            send(*table[name]).start()

    def arrive(p, chunk, h):
        piece = kbuf.at[p, chunk, pl.ds(h * hr, hr)]
        pltpu.make_async_copy(piece, piece, kr.at[p, chunk, h]).wait()

    arrive(0, rep, 0)
    arrive(0, rep, 1)
    start(0, "r0", "l1", "s0", "s1")

    def send_query(k, carry):
        peer = (dom + k) % nd
        pltpu.make_async_remote_copy(
            src_ref=outbox.at[:, peer],
            dst_ref=inbox.at[:, dom],
            send_sem=qs,
            recv_sem=qr,
            device_id=(peer, rep),
            device_id_type=MESH,
        ).start()
        return carry

    pltpu.make_async_copy(outbox.at[:, dom], inbox.at[:, dom], qr).start()
    lax.fori_loop(1, nd, send_query, 0)
    start(0, "r1", "l0")

    def send_label(k, carry):
        pltpu.make_async_remote_copy(
            src_ref=labels_ref,
            dst_ref=lab.at[rep],
            send_sem=ls,
            recv_sem=lr,
            device_id=(dom, (rep + k) % nrep),
            device_id_type=MESH,
        ).start()
        return carry

    lax.fori_loop(1, nrep, send_label, 0)
    arrive(1, rep, 0)
    arrive(1, rep, 1)
    start(1, "s0", "s1")

    log2e = math.log2(math.e) * (q_ref.shape[1] ** -0.5)

    def unit(p, chunk, h):
        keys = kbuf[p, chunk, pl.ds(h * hr, hr), :]
        named = lab[chunk, p : p + 1, pl.ds(pl.multiple_of(h * hr, hr), hr)]
        onehot = jnp.where(
            lax.broadcasted_iota(jnp.int32, (NCLASS, hr), 0) == named, 1.0, 0.0
        ).astype(jnp.bfloat16)
        bs = min(half, 256)
        for b in range(half // bs):
            at = pl.ds(b * bs, bs)
            doms = pl.ds(b * bs // CAP, bs // CAP)
            queries = inbox[p, doms].reshape(bs, -1)
            scores = lax.dot_general(queries, keys, NT, preferred_element_type=jnp.float32)
            m_old = m_s[at, :]
            m_new = jnp.maximum(m_old, jnp.max(scores, axis=1, keepdims=True))
            m_s[at, :] = m_new
            fade = jnp.exp2((m_old - m_new) * log2e)
            weights = jnp.exp2((scores - m_new[:, :1]) * log2e)
            high = weights.astype(jnp.bfloat16)
            low = (weights - high.astype(jnp.float32)).astype(jnp.bfloat16)
            sums = lax.dot_general(high, onehot, NT, preferred_element_type=jnp.float32)
            sums += lax.dot_general(low, onehot, NT, preferred_element_type=jnp.float32)
            old = acc[p, doms].reshape(bs, NCLASS)
            acc[p, doms] = (old * fade + sums).reshape(bs // CAP, CAP, NCLASS)

    def loop4(fn):
        def body(j, carry):
            fn(j)
            return carry

        lax.fori_loop(0, 4, body, 0)

    def own_units(p, ready):
        def fn(j):
            chunk = x * 2 + (c + j // 2) % 2
            if ready:
                pl.when(j >= 2)(lambda: arrive(p, chunk, j % 2))
            unit(p, chunk, j % 2)

        loop4(fn)

    def near_units(p, col, wait):
        def fn(j):
            chunk = ((x + nx - 1 + 2 * (j % 2)) % nx) * 2 + col
            h = ((j + 1) // 2) % 2
            if wait:
                arrive(p, chunk, h)
            unit(p, chunk, h)

        loop4(fn)

    def far_units(p):
        def fn(j):
            chunk = ((x + 2) % nx) * 2 + (c + j // 2) % 2
            pl.when(j >= 2)(lambda: arrive(p, chunk, j % 2))
            unit(p, chunk, j % 2)

        loop4(fn)

    def first_near(p):
        arrive(p, cl, 0)
        start(p, "rr", "sl0")
        arrive(p, cr, 1)
        start(p, "ll", "sr1")

    def second_near(p):
        arrive(p, cl, 1)
        arrive(p, cr, 0)
        start(p, "sl1", "sr0")

    def far(p):
        arrive(p, co, 0)
        start(p, "so0")
        arrive(p, co, 1)
        start(p, "so1")

    def reset(p):
        m_s[...] = jnp.full(m_s.shape, -3.0e38, jnp.float32)
        acc[p] = jnp.zeros(acc.shape[1:], jnp.float32)

    def send_back(p):
        def one(k, carry):
            peer = (dom + k) % nd
            pltpu.make_async_remote_copy(
                src_ref=acc.at[p, peer],
                dst_ref=ret.at[p, dom],
                send_sem=rs.at[p],
                recv_sem=rr.at[p],
                device_id=(peer, rep),
                device_id_type=MESH,
            ).start()
            return carry

        pltpu.make_async_copy(acc.at[p, dom], ret.at[p, dom], rr.at[p]).start()
        lax.fori_loop(1, nd, one, 0)
        lane = lax.broadcasted_iota(jnp.int32, (half, 128), 1) % CAP
        slot = lax.broadcasted_iota(jnp.int32, (half, 128), 0) % CAP
        diag = jnp.where(lane == slot, m_s[...], 0.0).reshape(nd, CAP, 128)
        mout[p] = jnp.sum(diag, axis=1, keepdims=True)

    def send_peaks():
        def one(k, carry):
            peer = (dom + k) % nd
            pltpu.make_async_remote_copy(
                src_ref=mout.at[:, peer],
                dst_ref=pin.at[:, dom],
                send_sem=ps,
                recv_sem=pr,
                device_id=(peer, rep),
                device_id_type=MESH,
            ).start()
            return carry

        pltpu.make_async_copy(mout.at[:, dom], pin.at[:, dom], pr).start()
        lax.fori_loop(1, nd, one, 0)

    first_near(0)
    second_near(0)
    start(1, "r0", "l1", "r1", "l0")
    reset(0)
    pltpu.make_async_copy(lab, lab, lr).wait()
    pltpu.make_async_copy(inbox, inbox, qr).wait()
    own_units(0, True)
    near_units(0, c, False)
    far(0)
    near_units(0, 1 - c, True)
    far_units(0)
    send_back(0)
    first_near(1)
    reset(1)
    own_units(1, True)
    second_near(1)
    near_units(1, c, False)
    near_units(1, 1 - c, True)
    far(1)
    far_units(1)
    send_back(1)
    send_peaks()

    for p in range(PARTS):
        for move in moves(p).values():
            send(*move).wait_send()
    others = pl.ds(0, nd - 1)
    pltpu.make_async_copy(outbox.at[:, others], outbox.at[:, others], qs).wait()
    few = pl.ds(0, nrep - 1)
    pltpu.make_async_copy(lab.at[few], lab.at[few], ls).wait()
    for p in range(PARTS):
        pltpu.make_async_copy(acc.at[p, others], acc.at[p, others], rs.at[p]).wait()
    pltpu.make_async_copy(mout.at[:, others], mout.at[:, others], ps).wait()

    pltpu.make_async_copy(pin, pin, pr).wait()
    pltpu.make_async_copy(ret.at[0], ret.at[0], rr.at[0]).wait()
    pltpu.make_async_copy(ret.at[1], ret.at[1], rr.at[1]).wait()
    nq = q_ref.shape[0]
    per = 128 // CAP
    gl = min(128, half)
    lane = lax.broadcasted_iota(jnp.int32, (1, 128), 1) // CAP
    peak_rows = []
    top = jnp.full((nq, 1), -3.0e38, jnp.float32)
    groups = [(p, g) for p in range(PARTS) for g in range(half // 128)]
    for p, g in groups:
        line = jnp.zeros((1, 128), jnp.float32)
        for i in range(per):
            line = jnp.where(lane == i, pin[p, g * per + i], line)
        peak_rows.append(line)
        chosen = mask[:, p * half + g * 128 : p * half + (g + 1) * 128] > 0.0
        top = jnp.maximum(top, jnp.max(jnp.where(chosen, line, -3.0e38), axis=1, keepdims=True))
    total = jnp.zeros((nq, NCLASS), jnp.float32)
    for (p, g), line in zip(groups, peak_rows):
        chosen = mask[:, p * half + g * 128 : p * half + (g + 1) * 128] > 0.0
        factor = jnp.where(chosen, jnp.exp2(jnp.where(chosen, line - top, 0.0) * log2e), 0.0)
        block = ret[p, g * per : (g + 1) * per].reshape(128, NCLASS)
        total += jnp.dot(factor, block, precision=lax.Precision.HIGHEST, preferred_element_type=jnp.float32)
    out_ref[...] = NCLASS * total / jnp.sum(total, axis=1, keepdims=True)


def local(queries, probes, corpus, labels):
    nd = lax.axis_size("dom")
    nrep = lax.axis_size("rep")
    nq, depth = queries.shape
    rows = corpus.shape[1]
    half = nd * CAP
    vmem = pl.BlockSpec(memory_space=pltpu.VMEM)
    dma = pltpu.SemaphoreType.DMA
    return pl.pallas_call(
        functools.partial(kernel, nd, nrep // 2),
        out_shape=jax.ShapeDtypeStruct((nq, NCLASS), jnp.float32),
        in_specs=[vmem, vmem, pl.BlockSpec(memory_space=pl.ANY), vmem],
        out_specs=vmem,
        scratch_shapes=[
            pltpu.VMEM((nq, PARTS * half), jnp.float32),
            pltpu.VMEM((PARTS, nd, CAP, depth), jnp.bfloat16),
            pltpu.VMEM((PARTS, nd, CAP, depth), jnp.bfloat16),
            pltpu.VMEM((PARTS, nrep, rows, depth), jnp.bfloat16),
            pltpu.VMEM((nrep, PARTS, rows), jnp.int32),
            pltpu.VMEM((PARTS, nd, CAP, NCLASS), jnp.float32),
            pltpu.VMEM((half, 128), jnp.float32),
            pltpu.VMEM((PARTS, nd, 1, 128), jnp.float32),
            pltpu.VMEM((PARTS, nd, 1, 128), jnp.float32),
            pltpu.VMEM((PARTS, nd, CAP, NCLASS), jnp.float32),
            dma((PARTS, 14)),
            dma((PARTS, nrep, 2)),
            dma, dma, dma, dma,
            dma((PARTS,)),
            dma((PARTS,)),
            dma, dma,
        ],
        compiler_params=pltpu.CompilerParams(
            collective_id=0, has_side_effects=True, vmem_limit_bytes=48 * 1024 * 1024
        ),
    )(queries, probes, corpus, labels)


def solution(mesh):
    in_specs = (
        P(("dom", "rep"), None),
        P(("dom", "rep"), None),
        P("dom", "rep", None),
        P("dom", "rep"),
    )
    out_specs = P(("dom", "rep"), None)
    return jax.shard_map(local, mesh=mesh, in_specs=in_specs, out_specs=out_specs, check_vma=False)
```

time: 412 us -> 80.3 us (0.19); the launches traced: 404 us -> 80.1 us
  waiting for transfers between devices: 146 us -> 0 us
  Pallas kernels: 0 us -> 76.8 us
  matrix products: 74.3 us -> 0 us
  local copies, waits for them, and re-layouts: 66.3 us -> 3.31 us
  blocking collectives: 51.3 us -> 0 us
  starting transfers between devices: 36.5 us -> 0 us
  other arithmetic: 15.4 us -> 0 us
  between operations: 13.9 us -> 0.02 us
    all_to_all x4 -> x0, waiting for transfers between devices: 95.2 us -> none  [the longest x1 94.1 us: local(): lax.all_to_all(outbox, 'dom', split_axis=0, concat_axis=1, tiled=True)]
    pallas_call x0 -> x1, Pallas kernels: none -> 76.8 us  [local(): pl.pallas_call(functools.partial(kernel, nd, nrep // 2), out_shape=jax.Sh...]
    dot_general x48 -> x0, matrix products: 74.3 us -> none  [the longest x16 32.3 us: finish(): class_sums = jnp.dot(weights, one_hot, precision=lax.Precision.HIGHEST)]
    all_to_all x4 -> x0, starting transfers between devices: 36.4 us -> none  [the longest x1 10.1 us: local(): lax.all_to_all(outbox, 'dom', split_axis=0, concat_axis=1, tiled=True)]
    unnamed x26 -> x8, local copies, waits for them, and re-layouts: 38.7 us -> 3.31 us
    reduce_scatter x1 -> x0, waiting for transfers between devices: 30.5 us -> none  [local(): lax.psum_scatter(class_parts, 'rep', scatter_dimension=1, tiled=True)]
    all_gather x2 -> x0, blocking collectives: 28.9 us -> none  [the longest x1 16 us: local(): lax.all_gather(probes, 'rep', axis=0, tiled=True)]
    pmax x1 -> x0, blocking collectives: 22.4 us -> none  [local(): peaks = lax.pmax(jnp.stack(peak_list), 'rep')]
  transfers between devices with their start and end apart: 6 -> 0, of which waited for: 4 -> 0; matrix products, arithmetic and copies ran while one was open for 5% -> 0% of each run, Pallas kernels for 0% -> 0%
where the time goes in v1:
time: 80.3 us; the launch traced here: 80.1 us
  Pallas kernels  76.8 us (96%)
  local copies, waits for them, and re-layouts  3.31 us (4%)
    pallas_call x1, Pallas kernels, local(): pl.pallas_call(functools.partial(kernel, nd, nrep // 2), out_shape=jax.Sh...  76.8 us
    unnamed x8, local copies, waits for them, and re-layouts  3.31 us

profile of v1, /device:TPU:1, one launch (start us, length us, event | category | flops | bytes accessed | tf_op | source)
XLA Modules:
  0.0 80.1 jit_solution(12278312301622988022)
XLA Ops:
  0.0 0.0 copy-start.1
  0.0 0.8 copy.5.probes_ref
  0.8 0.0 copy-done.1
  0.8 0.0 copy-start
  0.8 1.2 %copy-done = bf16[2,1024,256]{2,1,0:T(8,128)(2,1)S(1)} copy-done((bf16[2,1024,256]{2,1,0:T(8,128)(2,1)S(1)}, bf16[2,1024,256]{2,1,0:T(8,128)(2,1)}, u32[]{:S(2)}) %copy-start) | copy-done | bytes 1048600
  2.0 0.0 copy-start.2
  2.0 0.7 copy-done.2
  2.7 76.8 %shard_map.46 = f32[64,128]{1,0:T(8,128)S(1)} custom-call(bf16[64,256]{1,0:T(8,128)(2,1)S(1)} %copy-done.1, s32[64,8]{1,0:T(8,128)S(1)} %copy.5.probes_ref, bf16[2,1024,256]{2,1,0:T(8,128)(2,1)S(1)} %copy-done, s32[2,1024]{1,0:T(2,128)S(1)} %copy-done.2), custom_call_target="tpu_custom_call" | custom-call | tf_op jit(solution)/shard_map/pallas_call | solution.py:356
  79.5 0.6 copy.7
Async XLA Ops:
  0.0 0.8 copy-start.1
  0.8 1.2 %copy-start = (bf16[2,1024,256]{2,1,0:T(8,128)(2,1)S(1)}, bf16[2,1024,256]{2,1,0:T(8,128)(2,1)}, u32[]{:S(2)}) copy-start(bf16[2,1024,256]{2,1,0:T(8,128)(2,1)} %corpus_ref.1) | copy-start | bytes 3145732
  2.0 0.7 copy-start.2

commit v2 on v0

v2 whole, which is shorter than its diff:
```python
import functools
import math

import jax
import jax.numpy as jnp
from jax import lax
from jax.experimental import pallas as pl
from jax.experimental.pallas import tpu as pltpu
from jax.sharding import PartitionSpec as P

NCLASS = 128
CAP = 16
PARTS = 2
WINDOW = 4
STEPS = 32767.0
MESH = pl.DeviceIdType.MESH
NT = (((1,), (1,)), ((), ()))


def select_slots(named, nd):
    npr, nq = named.shape
    nparts = PARTS * nd
    width = max(128, nparts)
    part_ids = lax.broadcasted_iota(jnp.int32, (width, nq), 0)
    match = jnp.zeros((width, nq), jnp.float32)
    for j in range(npr):
        match = jnp.where(named[j : j + 1, :] == part_ids, 1.0, match)
    row = lax.broadcasted_iota(jnp.int32, (nq, nq), 0)
    col = lax.broadcasted_iota(jnp.int32, (nq, nq), 1)
    earlier = jnp.where(row < col, 1.0, 0.0).astype(jnp.bfloat16)
    rank = jnp.dot(match.astype(jnp.bfloat16), earlier, preferred_element_type=jnp.float32)
    code = jnp.where(match > 0.0, rank, -1.0)
    slots = nparts * CAP
    half = nd * CAP
    slot_row = lax.broadcasted_iota(jnp.int32, (slots, width), 0)
    slot_part = PARTS * ((slot_row % half) // CAP) + slot_row // half
    spread = jnp.where(lax.broadcasted_iota(jnp.int32, (slots, width), 1) == slot_part, 1.0, 0.0)
    wide = jnp.dot(
        spread.astype(jnp.bfloat16), code.astype(jnp.bfloat16), preferred_element_type=jnp.float32
    )
    slot = (lax.broadcasted_iota(jnp.int32, (slots, nq), 0) % CAP).astype(jnp.float32)
    return jnp.where(wide == slot, 1.0, 0.0)


def kernel(
    nd, nx,
    q_hbm, probes_hbm, corpus_hbm, labels_hbm, out_ref,
    q_ref, probes_ref, mask, outbox, inbox, kbuf, lab, acc, m_s, wire, mout, pin, ret,
    fs, ko, so_s, so_r, ks, kr, bs_s, bs_r, qs, qr, ls, lr, rs, rr, ps, pr,
):
    dom = lax.axis_index("dom")
    rep = lax.axis_index("rep")
    nrep = 2 * nx
    x, c = rep // 2, rep % 2
    rows = kbuf.shape[2]
    qrows = rows // 4
    half = nd * CAP
    nz = min(nd, 8)
    ny = nd // nz
    y, z = dom // nz, dom % nz
    right = (dom, ((x + 1) % nx) * 2 + c)
    left = (dom, ((x + nx - 1) % nx) * 2 + c)
    sibling = (dom, x * 2 + (1 - c))

    barrier = pltpu.get_barrier_semaphore()

    def greet_dom(k, carry):
        pl.semaphore_signal(barrier, inc=1, device_id=((dom + k) % nd, rep), device_id_type=MESH)
        return carry

    def greet_rep(k, carry):
        pl.semaphore_signal(barrier, inc=1, device_id=(dom, (rep + k) % nrep), device_id_type=MESH)
        return carry

    lax.fori_loop(1, nrep, greet_rep, 0)
    lax.fori_loop(1, nd, greet_dom, 0)

    get_probes = pltpu.make_async_copy(probes_hbm, probes_ref, fs.at[0])
    get_queries = pltpu.make_async_copy(q_hbm, q_ref, fs.at[1])
    get_labels = pltpu.make_async_copy(labels_hbm, lab.at[rep], fs.at[2])
    get_rows = [
        pltpu.make_async_copy(corpus_hbm.at[p], kbuf.at[p, rep], ko.at[p]) for p in range(PARTS)
    ]
    for copy in (get_probes, get_queries, get_rows[0], get_labels, get_rows[1]):
        copy.start()
    get_rows[0].wait()

    pl.semaphore_wait(barrier, nd - 1 + nrep - 1)

    def piece(p, xx, col, quarter):
        return kbuf.at[p, xx * 2 + col, pl.ds(pl.multiple_of(quarter * qrows, qrows), qrows)]

    def ring(way, g):
        p, k = g // 6, g % 6
        if way == 0:
            ref = piece(p, (x + nx - k // 4) % nx, c, k % 4)
        else:
            ref = piece(p, (x + k // 4) % nx, c, 3 - k % 4)
        return pltpu.make_async_remote_copy(
            src_ref=ref, dst_ref=ref, send_sem=ks.at[way, g], recv_sem=kr.at[way, g],
            device_id=right if way == 0 else left, device_id_type=MESH,
        )

    def landed(way, g, col):
        p, k = g // 6, g % 6
        if way == 0:
            return p, (x + 2 * nx - 1 - k // 4) % nx, col, k % 4
        return p, (x + 1 + k // 4) % nx, col, 3 - k % 4

    def share(way, g):
        ref = piece(*landed(way, g, c))
        return pltpu.make_async_remote_copy(
            src_ref=ref, dst_ref=ref, send_sem=bs_s.at[way, g], recv_sem=bs_r.at[way, g],
            device_id=sibling, device_id_type=MESH,
        )

    def share_own(p):
        ref = kbuf.at[p, rep]
        return pltpu.make_async_remote_copy(
            src_ref=ref, dst_ref=ref, send_sem=so_s.at[p], recv_sem=so_r.at[p],
            device_id=sibling, device_id_type=MESH,
        )

    for g in range(WINDOW):
        ring(0, g).start()
        ring(1, g).start()

    get_probes.wait()
    get_queries.wait()
    sel = select_slots(probes_ref[...], nd)
    picked = jnp.dot(sel.astype(jnp.bfloat16), q_ref[...], preferred_element_type=jnp.float32)
    outbox[...] = picked.astype(jnp.bfloat16).reshape(outbox.shape)
    get_labels.wait()
    get_rows[1].wait()


    def peer_of(t):
        i, j = t // ny, t % ny
        dz = nz // 2 + (1 - 2 * (i % 2)) * ((i + 1) // 2)
        dy = ny // 2 + (1 - 2 * (j % 2)) * ((j + 1) // 2)
        return ((y + dy) % ny) * nz + (z + dz) % nz

    def to_all(src, dst, send_sem, recv_sem):
        def one(t, carry):
            peer = peer_of(t)
            pltpu.make_async_remote_copy(
                src_ref=src(peer), dst_ref=dst(dom), send_sem=send_sem, recv_sem=recv_sem,
                device_id=(peer, rep), device_id_type=MESH,
            ).start()
            return carry

        lax.fori_loop(0, nd - 1, one, 0)
        pltpu.make_async_copy(src(dom), dst(dom), recv_sem).start()

    to_all(lambda d: outbox.at[:, d], lambda d: inbox.at[:, d], qs, qr)

    def send_label(k, carry):
        pltpu.make_async_remote_copy(
            src_ref=lab.at[rep], dst_ref=lab.at[rep], send_sem=ls, recv_sem=lr,
            device_id=(dom, (rep + k) % nrep), device_id_type=MESH,
        ).start()
        return carry

    lax.fori_loop(1, nrep, send_label, 0)
    share_own(0).start()

    def event(g):
        for way in range(2):
            ref = piece(*landed(way, g, c))
            pltpu.make_async_copy(ref, ref, kr.at[way, g]).wait()
            share(way, g).start()

        @pl.when(g + WINDOW < 12)
        def _():
            ring(0, g + WINDOW).start()
            ring(1, g + WINDOW).start()

    log2e = math.log2(math.e) * (q_ref.shape[1] ** -0.5)

    def unit(p, pieces):
        queries = inbox[p].reshape(half, -1)
        scores, onehots = [], []
        for _, xx, col, quarter in pieces:
            at = pl.ds(pl.multiple_of(quarter * qrows, qrows), qrows)
            keys = kbuf[p, xx * 2 + col, at, :]
            named = lab[xx * 2 + col, p : p + 1, at]
            classes = lax.broadcasted_iota(jnp.int32, (NCLASS, qrows), 0)
            onehots.append(jnp.where(classes == named, 1.0, 0.0).astype(jnp.bfloat16))
            scores.append(lax.dot_general(queries, keys, NT, preferred_element_type=jnp.float32))
        scores = jnp.concatenate(scores, axis=1)
        m_old = m_s[...]
        m_new = jnp.maximum(m_old, jnp.max(scores, axis=1, keepdims=True))
        m_s[...] = m_new
        fade = jnp.exp2((m_old - m_new) * log2e)
        wide = jnp.concatenate([m_new] * (scores.shape[1] // 128), axis=1)
        weights = jnp.exp2((scores - wide) * log2e)
        high = weights.astype(jnp.bfloat16)
        low = (weights - high.astype(jnp.float32)).astype(jnp.bfloat16)
        sums = lax.dot_general(
            jnp.concatenate([high, low], axis=1), jnp.concatenate(onehots * 2, axis=1), NT,
            preferred_element_type=jnp.float32,
        )
        acc[...] = acc[...] * fade + sums

    def own_units(p):
        m_s[...] = jnp.full(m_s.shape, -3.0e38, jnp.float32)
        acc[...] = jnp.zeros(acc.shape, jnp.float32)

        def body(i, carry):
            col = (c + i) % 2

            @pl.when(i == 1)
            def _():
                ref = kbuf.at[p, x * 2 + col]
                pltpu.make_async_copy(ref, ref, so_r.at[p]).wait()

            unit(p, [(p, x, col, quarter) for quarter in range(4)])
            return carry

        lax.fori_loop(0, 2, body, 0)

    def here(g):
        return [landed(way, g, c) for way in range(2)]

    def there(g):
        pieces = [landed(way, g, 1 - c) for way in range(2)]
        for way in range(2):
            ref = piece(*pieces[way])
            pltpu.make_async_copy(ref, ref, bs_r.at[way, g]).wait()
        return pieces

    def finish(p):
        lane = lax.broadcasted_iota(jnp.int32, (half, 128), 1) % CAP
        slot = lax.broadcasted_iota(jnp.int32, (half, 128), 0) % CAP
        diag = jnp.where(lane == slot, m_s[...], 0.0).reshape(nd, CAP, 128)
        mout[p, :, 0] = jnp.sum(diag, axis=1, keepdims=True)
        sums = acc[...]
        most = jnp.max(sums, axis=1, keepdims=True)
        diag = jnp.where(lane == slot, most, 0.0).reshape(nd, CAP, 128)
        mout[p, :, 1] = jnp.sum(diag, axis=1, keepdims=True)
        codes = jnp.round(sums * (STEPS / most)).astype(jnp.int32).astype(jnp.int16)
        wire[p] = codes.reshape(nd, CAP, NCLASS)

    def send_back(p):
        to_all(lambda d: wire.at[p, d], lambda d: ret.at[p, d], rs.at[p], rr.at[p])
        to_all(lambda d: mout.at[p, d], lambda d: pin.at[p, d], ps.at[p], pr.at[p])

    event(0)
    event(1)
    mask[...] = sel.T
    pltpu.make_async_copy(lab.at[pl.ds(0, nrep - 1)], lab.at[pl.ds(0, nrep - 1)], lr).wait()
    pltpu.make_async_copy(inbox, inbox, qr).wait()
    own_units(0)
    share_own(1).start()

    def first(g, carry):
        event(g + 2)
        unit(0, here(g) + there(g))
        return carry

    lax.fori_loop(0, 6, first, 0)
    finish(0)
    send_back(0)
    own_units(1)

    def second(g, carry):
        pl.when(g > 6)(lambda: event(g + 1))
        unit(1, here(g) + there(g))
        return carry

    lax.fori_loop(6, 11, second, 0)
    unit(1, here(11))
    unit(1, there(11))
    finish(1)
    send_back(1)

    def gone(g, carry):
        for way in range(2):
            ring(way, g).wait_send()
            share(way, g).wait_send()
        return carry

    lax.fori_loop(0, 12, gone, 0)
    for p in range(PARTS):
        share_own(p).wait_send()
    others = pl.ds(0, nd - 1)
    few = pl.ds(0, nrep - 1)
    pltpu.make_async_copy(outbox.at[:, others], outbox.at[:, others], qs).wait()
    pltpu.make_async_copy(lab.at[few], lab.at[few], ls).wait()

    def left_home(p):
        pltpu.make_async_copy(wire.at[p, others], wire.at[p, others], rs.at[p]).wait()
        pltpu.make_async_copy(mout.at[p, others], mout.at[p, others], ps.at[p]).wait()

    left_home(0)

    nq = q_ref.shape[0]
    per = 128 // CAP
    lane = lax.broadcasted_iota(jnp.int32, (1, 128), 1) // CAP
    top = jnp.full((nq, 1), -3.0e38, jnp.float32)
    total = jnp.zeros((nq, NCLASS), jnp.float32)
    for p in range(PARTS):
        pltpu.make_async_copy(pin.at[p], pin.at[p], pr.at[p]).wait()
        found = []
        new_top = top
        for g in range(half // 128):
            line = jnp.zeros((1, 128), jnp.float32)
            most = jnp.zeros((1, 128), jnp.float32)
            for i in range(per):
                line = jnp.where(lane == i, pin[p, g * per + i, 0], line)
                most = jnp.where(lane == i, pin[p, g * per + i, 1], most)
            chosen = mask[:, p * half + g * 128 : p * half + (g + 1) * 128] > 0.0
            found.append((chosen, line, most))
            best = jnp.max(jnp.where(chosen, line, -3.0e38), axis=1, keepdims=True)
            new_top = jnp.maximum(new_top, best)
        total = total * jnp.exp2((top - new_top) * log2e)
        top = new_top
        factors = [
            jnp.where(chosen, jnp.exp2(jnp.where(chosen, line - top, 0.0) * log2e) * (most / STEPS), 0.0)
            for chosen, line, most in found
        ]
        pltpu.make_async_copy(ret.at[p], ret.at[p], rr.at[p]).wait()
        for g, factor in enumerate(factors):
            block = ret[p, g * per : (g + 1) * per].astype(jnp.int32).astype(jnp.float32).reshape(128, NCLASS)
            total += jnp.dot(factor, block, precision=lax.Precision.HIGHEST, preferred_element_type=jnp.float32)
    out_ref[...] = NCLASS * total / jnp.sum(total, axis=1, keepdims=True)
    left_home(1)


def local(queries, probes, corpus, labels):
    nd = lax.axis_size("dom")
    nrep = lax.axis_size("rep")
    nq, depth = queries.shape
    rows = corpus.shape[1]
    half = nd * CAP
    dma = pltpu.SemaphoreType.DMA
    return pl.pallas_call(
        functools.partial(kernel, nd, nrep // 2),
        out_shape=jax.ShapeDtypeStruct((nq, NCLASS), jnp.float32),
        in_specs=[pl.BlockSpec(memory_space=pl.ANY)] * 4,
        out_specs=pl.BlockSpec(memory_space=pltpu.VMEM),
        scratch_shapes=[
            pltpu.VMEM((nq, depth), jnp.bfloat16),
            pltpu.VMEM((probes.shape[1], nq), jnp.int32),
            pltpu.VMEM((nq, PARTS * half), jnp.float32),
            pltpu.VMEM((PARTS, nd, CAP, depth), jnp.bfloat16),
            pltpu.VMEM((PARTS, nd, CAP, depth), jnp.bfloat16),
            pltpu.VMEM((PARTS, nrep, rows, depth), jnp.bfloat16),
            pltpu.VMEM((nrep, PARTS, rows), jnp.int32),
            pltpu.VMEM((half, NCLASS), jnp.float32),
            pltpu.VMEM((half, 128), jnp.float32),
            pltpu.VMEM((PARTS, nd, CAP, NCLASS), jnp.int16),
            pltpu.VMEM((PARTS, nd, 2, 1, 128), jnp.float32),
            pltpu.VMEM((PARTS, nd, 2, 1, 128), jnp.float32),
            pltpu.VMEM((PARTS, nd, CAP, NCLASS), jnp.int16),
            dma((3,)),
            dma((PARTS,)),
            dma((PARTS,)),
            dma((PARTS,)),
            dma((2, 12)),
            dma((2, 12)),
            dma((2, 12)),
            dma((2, 12)),
            dma, dma, dma, dma,
            dma((PARTS,)),
            dma((PARTS,)),
            dma((PARTS,)),
            dma((PARTS,)),
        ],
        compiler_params=pltpu.CompilerParams(
            collective_id=0, has_side_effects=True, vmem_limit_bytes=62 * 1024 * 1024
        ),
    )(queries, probes.T, corpus, labels)


def solution(mesh):
    in_specs = (
        P(("dom", "rep"), None),
        P(("dom", "rep"), None),
        P("dom", "rep", None),
        P("dom", "rep"),
    )
    out_specs = P(("dom", "rep"), None)
    return jax.shard_map(local, mesh=mesh, in_specs=in_specs, out_specs=out_specs, check_vma=False)
```

time: 412 us -> 63.6 us (0.15); the launches traced: 404 us -> 63.4 us
  waiting for transfers between devices: 146 us -> 0 us
  matrix products: 74.3 us -> 0 us
  local copies, waits for them, and re-layouts: 66.3 us -> 1.38 us
  Pallas kernels: 0 us -> 62 us
  blocking collectives: 51.3 us -> 0 us
  starting transfers between devices: 36.5 us -> 0 us
  other arithmetic: 15.4 us -> 0 us
  between operations: 13.9 us -> 0.01 us
    all_to_all x4 -> x0, waiting for transfers between devices: 95.2 us -> none  [the longest x1 94.1 us: local(): lax.all_to_all(outbox, 'dom', split_axis=0, concat_axis=1, tiled=True)]
    dot_general x48 -> x0, matrix products: 74.3 us -> none  [the longest x16 32.3 us: finish(): class_sums = jnp.dot(weights, one_hot, precision=lax.Precision.HIGHEST)]
    pallas_call x0 -> x1, Pallas kernels: none -> 62 us  [local(): pl.pallas_call(functools.partial(kernel, nd, nrep // 2), out_shape=jax.Sh...]
    unnamed x26 -> x1, local copies, waits for them, and re-layouts: 38.7 us -> 1.38 us
    all_to_all x4 -> x0, starting transfers between devices: 36.4 us -> none  [the longest x1 10.1 us: local(): lax.all_to_all(outbox, 'dom', split_axis=0, concat_axis=1, tiled=True)]
    reduce_scatter x1 -> x0, waiting for transfers between devices: 30.5 us -> none  [local(): lax.psum_scatter(class_parts, 'rep', scatter_dimension=1, tiled=True)]
    all_gather x2 -> x0, blocking collectives: 28.9 us -> none  [the longest x1 16 us: local(): lax.all_gather(probes, 'rep', axis=0, tiled=True)]
    pmax x1 -> x0, blocking collectives: 22.4 us -> none  [local(): peaks = lax.pmax(jnp.stack(peak_list), 'rep')]
  transfers between devices with their start and end apart: 6 -> 0, of which waited for: 4 -> 0; matrix products, arithmetic and copies ran while one was open for 5% -> 0% of each run, Pallas kernels for 0% -> 0%
where the time goes in v2:
time: 63.6 us; the launch traced here: 63.4 us
  Pallas kernels  62 us (97%)
  local copies, waits for them, and re-layouts  1.38 us (2%)
    pallas_call x1, Pallas kernels, local(): pl.pallas_call(functools.partial(kernel, nd, nrep // 2), out_shape=jax.Sh...  62 us
    unnamed x1, local copies, waits for them, and re-layouts  1.38 us

profile of v2, /device:TPU:1, one launch (start us, length us, event | category | flops | bytes accessed | tf_op | source)
XLA Modules:
  0.0 63.4 jit_solution(8194869673402674849)
XLA Ops:
  0.0 62.0 %shard_map.46 = f32[64,128]{1,0:T(8,128)} custom-call(bf16[64,256]{1,0:T(8,128)(2,1)} %q_hbm.1, s32[8,64]{1,0:T(8,128)} %bitcast.1, bf16[2,1024,256]{2,1,0:T(8,128)(2,1)} %corpus_hbm.1, s32[2,1024]{1,0:T(2,128)} %labels_hbm.1), custom_call_target="tpu_custom_call" | custom-call | tf_op jit(solution)/shard_map/pallas_call | solution.py:337
  62.0 1.4 %copy.6 = f32[64,128]{1,0:T(8,128)} copy(f32[64,128]{1,0:T(8,128)} %shard_map.46) | data formatting | bytes 65536

commit v3 on v2

--- a/solution.py
+++ b/solution.py
@@ -51,29 +51,41 @@
     dom = lax.axis_index("dom")
     rep = lax.axis_index("rep")
     nrep = 2 * nx
-    x, c = rep // 2, rep % 2
+    x, c = lax.div(rep, 2), lax.rem(rep, 2)
     rows = kbuf.shape[2]
     qrows = rows // 4
     half = nd * CAP
     nz = min(nd, 8)
     ny = nd // nz
-    y, z = dom // nz, dom % nz
-    right = (dom, ((x + 1) % nx) * 2 + c)
-    left = (dom, ((x + nx - 1) % nx) * 2 + c)
+    y, z = lax.div(dom, nz), lax.rem(dom, nz)
+    right = (dom, lax.rem(x + 1, nx) * 2 + c)
+    left = (dom, lax.rem(x + nx - 1, nx) * 2 + c)
     sibling = (dom, x * 2 + (1 - c))
 
+    lines = [
+        lax.rem(y + (ny // 2 + (1 - 2 * (j % 2)) * ((j + 1) // 2)), ny) * nz for j in range(ny)
+    ]
+
+    def each_peer(act):
+        def one(i, carry):
+            dz = nz // 2 + (1 - 2 * lax.rem(i, 2)) * lax.div(i + 1, 2)
+            there = lax.rem(z + dz, nz)
+            for line in lines:
+                act(line + there)
+            return carry
+
+        lax.fori_loop(0, nz - 1, one, 0)
+        for line in lines[:-1]:
+            act(line + z)
+
     barrier = pltpu.get_barrier_semaphore()
 
-    def greet_dom(k, carry):
-        pl.semaphore_signal(barrier, inc=1, device_id=((dom + k) % nd, rep), device_id_type=MESH)
-        return carry
-
-    def greet_rep(k, carry):
-        pl.semaphore_signal(barrier, inc=1, device_id=(dom, (rep + k) % nrep), device_id_type=MESH)
-        return carry
-
-    lax.fori_loop(1, nrep, greet_rep, 0)
-    lax.fori_loop(1, nd, greet_dom, 0)
+    def greet(device):
+        pl.semaphore_signal(barrier, inc=1, device_id=device, device_id_type=MESH)
+
+    each_peer(lambda peer: greet((peer, rep)))
+    for k in range(1, nrep):
+        greet((dom, lax.rem(rep + k, nrep)))
 
     get_probes = pltpu.make_async_copy(probes_hbm, probes_ref, fs.at[0])
     get_queries = pltpu.make_async_copy(q_hbm, q_ref, fs.at[1])
@@ -91,21 +103,21 @@
         return kbuf.at[p, xx * 2 + col, pl.ds(pl.multiple_of(quarter * qrows, qrows), qrows)]
 
     def ring(way, g):
-        p, k = g // 6, g % 6
+        p, k = lax.div(g, 6), lax.rem(g, 6)
         if way == 0:
-            ref = piece(p, (x + nx - k // 4) % nx, c, k % 4)
+            ref = piece(p, lax.rem(x + nx - lax.div(k, 4), nx), c, lax.rem(k, 4))
         else:
-            ref = piece(p, (x + k // 4) % nx, c, 3 - k % 4)
+            ref = piece(p, lax.rem(x + lax.div(k, 4), nx), c, 3 - lax.rem(k, 4))
         return pltpu.make_async_remote_copy(
             src_ref=ref, dst_ref=ref, send_sem=ks.at[way, g], recv_sem=kr.at[way, g],
             device_id=right if way == 0 else left, device_id_type=MESH,
         )
 
     def landed(way, g, col):
-        p, k = g // 6, g % 6
+        p, k = lax.div(g, 6), lax.rem(g, 6)
         if way == 0:
-            return p, (x + 2 * nx - 1 - k // 4) % nx, col, k % 4
-        return p, (x + 1 + k // 4) % nx, col, 3 - k % 4
+            return p, lax.rem(x + 2 * nx - 1 - lax.div(k, 4), nx), col, lax.rem(k, 4)
+        return p, lax.rem(x + 1 + lax.div(k, 4), nx), col, 3 - lax.rem(k, 4)
 
     def share(way, g):
         ref = piece(*landed(way, g, c))
@@ -134,34 +146,23 @@
     get_rows[1].wait()
 
 
-    def peer_of(t):
-        i, j = t // ny, t % ny
-        dz = nz // 2 + (1 - 2 * (i % 2)) * ((i + 1) // 2)
-        dy = ny // 2 + (1 - 2 * (j % 2)) * ((j + 1) // 2)
-        return ((y + dy) % ny) * nz + (z + dz) % nz
-
     def to_all(src, dst, send_sem, recv_sem):
-        def one(t, carry):
-            peer = peer_of(t)
+        def send(peer):
             pltpu.make_async_remote_copy(
                 src_ref=src(peer), dst_ref=dst(dom), send_sem=send_sem, recv_sem=recv_sem,
                 device_id=(peer, rep), device_id_type=MESH,
             ).start()
-            return carry
-
-        lax.fori_loop(0, nd - 1, one, 0)
+
+        each_peer(send)
         pltpu.make_async_copy(src(dom), dst(dom), recv_sem).start()
 
     to_all(lambda d: outbox.at[:, d], lambda d: inbox.at[:, d], qs, qr)
 
-    def send_label(k, carry):
+    for k in range(1, nrep):
         pltpu.make_async_remote_copy(
             src_ref=lab.at[rep], dst_ref=lab.at[rep], send_sem=ls, recv_sem=lr,
-            device_id=(dom, (rep + k) % nrep), device_id_type=MESH,
+            device_id=(dom, lax.rem(rep + k, nrep)), device_id_type=MESH,
         ).start()
-        return carry
-
-    lax.fori_loop(1, nrep, send_label, 0)
     share_own(0).start()
 
     def event(g):
@@ -183,14 +184,14 @@
         for _, xx, col, quarter in pieces:
             at = pl.ds(pl.multiple_of(quarter * qrows, qrows), qrows)
             keys = kbuf[p, xx * 2 + col, at, :]
-            named = lab[xx * 2 + col, p : p + 1, at]
+            named = lab[xx * 2 + col, pl.ds(p, 1), at]
             classes = lax.broadcasted_iota(jnp.int32, (NCLASS, qrows), 0)
             onehots.append(jnp.where(classes == named, 1.0, 0.0).astype(jnp.bfloat16))
             scores.append(lax.dot_general(queries, keys, NT, preferred_element_type=jnp.float32))
         scores = jnp.concatenate(scores, axis=1)
-        m_old = m_s[...]
+        m_old = m_s[p]
         m_new = jnp.maximum(m_old, jnp.max(scores, axis=1, keepdims=True))
-        m_s[...] = m_new
+        m_s[p] = m_new
         fade = jnp.exp2((m_old - m_new) * log2e)
         wide = jnp.concatenate([m_new] * (scores.shape[1] // 128), axis=1)
         weights = jnp.exp2((scores - wide) * log2e)
@@ -200,41 +201,53 @@
             jnp.concatenate([high, low], axis=1), jnp.concatenate(onehots * 2, axis=1), NT,
             preferred_element_type=jnp.float32,
         )
-        acc[...] = acc[...] * fade + sums
-
-    def own_units(p):
-        m_s[...] = jnp.full(m_s.shape, -3.0e38, jnp.float32)
-        acc[...] = jnp.zeros(acc.shape, jnp.float32)
-
-        def body(i, carry):
-            col = (c + i) % 2
-
-            @pl.when(i == 1)
-            def _():
-                ref = kbuf.at[p, x * 2 + col]
-                pltpu.make_async_copy(ref, ref, so_r.at[p]).wait()
-
-            unit(p, [(p, x, col, quarter) for quarter in range(4)])
-            return carry
-
-        lax.fori_loop(0, 2, body, 0)
-
-    def here(g):
-        return [landed(way, g, c) for way in range(2)]
-
-    def there(g):
-        pieces = [landed(way, g, 1 - c) for way in range(2)]
+        acc[p] = acc[p] * fade + sums
+
+    def own_unit(t, carry):
+        p, i = lax.div(t, 2), lax.rem(t, 2)
+        col = lax.rem(c + i, 2)
+        pl.when(t >= 2)(lambda: event(t + 1))
+
+        @pl.when(i == 1)
+        def _():
+            ref = kbuf.at[p, x * 2 + col]
+            pltpu.make_async_copy(ref, ref, so_r.at[p]).wait()
+
+        unit(p, [(p, x, col, quarter) for quarter in range(4)])
+        return carry
+
+    def passed(g):
         for way in range(2):
-            ref = piece(*pieces[way])
+            ref = piece(*landed(way, g, 1 - c))
             pltpu.make_async_copy(ref, ref, bs_r.at[way, g]).wait()
-        return pieces
+
+    def ring_unit(g, carry):
+        pl.when(g == 1)(lambda: event(5))
+        pl.when(g == 4)(lambda: event(6))
+        pl.when(g >= 6)(lambda: event(g + 1))
+
+        @pl.when(g == 6)
+        def _():
+            finish(0)
+            send_back(0)
+
+        passed(g)
+        unit(lax.div(g, 6), [landed(way, g, col) for col in (c, 1 - c) for way in range(2)])
+        return carry
+
+    def last_unit(t, carry):
+        g, i = 10 + lax.div(t, 2), lax.rem(t, 2)
+        pl.when(t == 1)(lambda: event(11))
+        pl.when(i == 1)(lambda: passed(g))
+        unit(PARTS - 1, [landed(way, g, lax.rem(c + i, 2)) for way in range(2)])
+        return carry
 
     def finish(p):
         lane = lax.broadcasted_iota(jnp.int32, (half, 128), 1) % CAP
         slot = lax.broadcasted_iota(jnp.int32, (half, 128), 0) % CAP
-        diag = jnp.where(lane == slot, m_s[...], 0.0).reshape(nd, CAP, 128)
+        diag = jnp.where(lane == slot, m_s[p], 0.0).reshape(nd, CAP, 128)
         mout[p, :, 0] = jnp.sum(diag, axis=1, keepdims=True)
-        sums = acc[...]
+        sums = acc[p]
         most = jnp.max(sums, axis=1, keepdims=True)
         diag = jnp.where(lane == slot, most, 0.0).reshape(nd, CAP, 128)
         mout[p, :, 1] = jnp.sum(diag, axis=1, keepdims=True)
@@ -247,30 +260,16 @@
 
     event(0)
     event(1)
+    share_own(1).start()
+    m_s[...] = jnp.full(m_s.shape, -3.0e38, jnp.float32)
+    acc[...] = jnp.zeros(acc.shape, jnp.float32)
     mask[...] = sel.T
     pltpu.make_async_copy(lab.at[pl.ds(0, nrep - 1)], lab.at[pl.ds(0, nrep - 1)], lr).wait()
+    event(2)
     pltpu.make_async_copy(inbox, inbox, qr).wait()
-    own_units(0)
-    share_own(1).start()
-
-    def first(g, carry):
-        event(g + 2)
-        unit(0, here(g) + there(g))
-        return carry
-
-    lax.fori_loop(0, 6, first, 0)
-    finish(0)
-    send_back(0)
-    own_units(1)
-
-    def second(g, carry):
-        pl.when(g > 6)(lambda: event(g + 1))
-        unit(1, here(g) + there(g))
-        return carry
-
-    lax.fori_loop(6, 11, second, 0)
-    unit(1, here(11))
-    unit(1, there(11))
+    lax.fori_loop(0, 4, own_unit, 0)
+    lax.fori_loop(0, 10, ring_unit, 0)
+    lax.fori_loop(0, 4, last_unit, 0)
     finish(1)
     send_back(1)
 
@@ -320,9 +319,11 @@
             for chosen, line, most in found
         ]
         pltpu.make_async_copy(ret.at[p], ret.at[p], rr.at[p]).wait()
-        for g, factor in enumerate(factors):
-            block = ret[p, g * per : (g + 1) * per].astype(jnp.int32).astype(jnp.float32).reshape(128, NCLASS)
-            total += jnp.dot(factor, block, precision=lax.Precision.HIGHEST, preferred_element_type=jnp.float32)
+        codes = ret[p].astype(jnp.int32).astype(jnp.float32).reshape(half, NCLASS)
+        total += jnp.dot(
+            jnp.concatenate(factors, axis=1), codes,
+            precision=lax.Precision.HIGHEST, preferred_element_type=jnp.float32,
+        )
     out_ref[...] = NCLASS * total / jnp.sum(total, axis=1, keepdims=True)
     left_home(1)
 
@@ -347,8 +348,8 @@
             pltpu.VMEM((PARTS, nd, CAP, depth), jnp.bfloat16),
             pltpu.VMEM((PARTS, nrep, rows, depth), jnp.bfloat16),
             pltpu.VMEM((nrep, PARTS, rows), jnp.int32),
-            pltpu.VMEM((half, NCLASS), jnp.float32),
-            pltpu.VMEM((half, 128), jnp.float32),
+            pltpu.VMEM((PARTS, half, NCLASS), jnp.float32),
+            pltpu.VMEM((PARTS, half, 128), jnp.float32),
             pltpu.VMEM((PARTS, nd, CAP, NCLASS), jnp.int16),
             pltpu.VMEM((PARTS, nd, 2, 1, 128), jnp.float32),
             pltpu.VMEM((PARTS, nd, 2, 1, 128), jnp.float32),

time: 63.6 us -> 60.8 us (0.956)
  Pallas kernels: 62 us -> 59.2 us
    pallas_call x1, Pallas kernels: 62 us -> 59.2 us  [local(): pl.pallas_call(functools.partial(kernel, nd, nrep // 2), out_shape=jax.Sh...]
where the time goes in v3:
time: 60.8 us; the launch traced here: 60.6 us
  Pallas kernels  59.2 us (97%)
  local copies, waits for them, and re-layouts  1.38 us (2%)
    pallas_call x1, Pallas kernels, local(): pl.pallas_call(functools.partial(kernel, nd, nrep // 2), out_shape=jax.Sh...  59.2 us
    unnamed x1, local copies, waits for them, and re-layouts  1.38 us

profile of v3, /device:TPU:1, one launch (start us, length us, event | category | flops | bytes accessed | tf_op | source)
XLA Modules:
  0.0 60.6 jit_solution(6422922737509548774)
XLA Ops:
  0.0 59.2 %shard_map.46 = f32[64,128]{1,0:T(8,128)} custom-call(bf16[64,256]{1,0:T(8,128)(2,1)} %q_hbm.1, s32[8,64]{1,0:T(8,128)} %bitcast.1, bf16[2,1024,256]{2,1,0:T(8,128)(2,1)} %corpus_hbm.1, s32[2,1024]{1,0:T(2,128)} %labels_hbm.1), custom_call_target="tpu_custom_call" | custom-call | tf_op jit(solution)/shard_map/pallas_call | solution.py:338
  59.2 1.4 %copy.6 = f32[64,128]{1,0:T(8,128)} copy(f32[64,128]{1,0:T(8,128)} %shard_map.46) | data formatting | bytes 65536

commit v4 on v3

--- a/solution.py
+++ b/solution.py
@@ -46,20 +46,21 @@
     nd, nx,
     q_hbm, probes_hbm, corpus_hbm, labels_hbm, out_ref,
     q_ref, probes_ref, mask, outbox, inbox, kbuf, lab, acc, m_s, wire, mout, pin, ret,
-    fs, ko, so_s, so_r, ks, kr, bs_s, bs_r, qs, qr, ls, lr, rs, rr, ps, pr,
+    fs, ko, so_s, so_r, ks, kr, bs_s, bs_r, ls_s, ls_r, lb_s, lb_r, qs, qr, ls, lr, ms, mr, rs, rr, ps, pr,
 ):
     dom = lax.axis_index("dom")
     rep = lax.axis_index("rep")
-    nrep = 2 * nx
     x, c = lax.div(rep, 2), lax.rem(rep, 2)
     rows = kbuf.shape[2]
     qrows = rows // 4
+    hrows = rows // 8
     half = nd * CAP
     nz = min(nd, 8)
     ny = nd // nz
     y, z = lax.div(dom, nz), lax.rem(dom, nz)
     right = (dom, lax.rem(x + 1, nx) * 2 + c)
     left = (dom, lax.rem(x + nx - 1, nx) * 2 + c)
+    across = (dom, lax.rem(x + 2, nx) * 2 + c)
     sibling = (dom, x * 2 + (1 - c))
 
     lines = [
@@ -83,9 +84,9 @@
     def greet(device):
         pl.semaphore_signal(barrier, inc=1, device_id=device, device_id_type=MESH)
 
+    for device in (sibling, right, left, across):
+        greet(device)
     each_peer(lambda peer: greet((peer, rep)))
-    for k in range(1, nrep):
-        greet((dom, lax.rem(rep + k, nrep)))
 
     get_probes = pltpu.make_async_copy(probes_hbm, probes_ref, fs.at[0])
     get_queries = pltpu.make_async_copy(q_hbm, q_ref, fs.at[1])
@@ -97,7 +98,7 @@
         copy.start()
     get_rows[0].wait()
 
-    pl.semaphore_wait(barrier, nd - 1 + nrep - 1)
+    pl.semaphore_wait(barrier, nd + 3)
 
     def piece(p, xx, col, quarter):
         return kbuf.at[p, xx * 2 + col, pl.ds(pl.multiple_of(quarter * qrows, qrows), qrows)]
@@ -126,6 +127,28 @@
             device_id=sibling, device_id_type=MESH,
         )
 
+    def halves(way, col):
+        p, xx, col, quarter = landed(way, 11, col)
+        return [
+            kbuf.at[p, xx * 2 + col, pl.ds(pl.multiple_of(quarter * qrows + j * hrows, hrows), hrows)]
+            for j in range(2)
+        ]
+
+    def last_ring(way, j):
+        p, xx, quarter = PARTS - 1, lax.rem(x + (nx - 1 if way == 0 else 1), nx), 1 if way == 0 else 2
+        ref = kbuf.at[p, xx * 2 + c, pl.ds(quarter * qrows + j * hrows, hrows)]
+        return pltpu.make_async_remote_copy(
+            src_ref=ref, dst_ref=ref, send_sem=ls_s.at[way, j], recv_sem=ls_r.at[way, j],
+            device_id=right if way == 0 else left, device_id_type=MESH,
+        )
+
+    def last_share(way, j):
+        ref = halves(way, c)[j]
+        return pltpu.make_async_remote_copy(
+            src_ref=ref, dst_ref=ref, send_sem=lb_s.at[way, j], recv_sem=lb_r.at[way, j],
+            device_id=sibling, device_id_type=MESH,
+        )
+
     def share_own(p):
         ref = kbuf.at[p, rep]
         return pltpu.make_async_remote_copy(
@@ -146,23 +169,30 @@
     get_rows[1].wait()
 
 
-    def to_all(src, dst, send_sem, recv_sem):
+    def to_all(*blocks):
         def send(peer):
-            pltpu.make_async_remote_copy(
-                src_ref=src(peer), dst_ref=dst(dom), send_sem=send_sem, recv_sem=recv_sem,
-                device_id=(peer, rep), device_id_type=MESH,
-            ).start()
+            for src, dst, send_sem, recv_sem in blocks:
+                pltpu.make_async_remote_copy(
+                    src_ref=src(peer), dst_ref=dst(dom), send_sem=send_sem, recv_sem=recv_sem,
+                    device_id=(peer, rep), device_id_type=MESH,
+                ).start()
 
         each_peer(send)
-        pltpu.make_async_copy(src(dom), dst(dom), recv_sem).start()
-
-    to_all(lambda d: outbox.at[:, d], lambda d: inbox.at[:, d], qs, qr)
-
-    for k in range(1, nrep):
+        for src, dst, _, recv_sem in blocks:
+            pltpu.make_async_copy(src(dom), dst(dom), recv_sem).start()
+
+    to_all((lambda d: outbox.at[:, d], lambda d: inbox.at[:, d], qs, qr))
+
+    def send_label(xx, device, send_sem, recv_sem):
+        ref = lab.at[xx * 2 + c]
         pltpu.make_async_remote_copy(
-            src_ref=lab.at[rep], dst_ref=lab.at[rep], send_sem=ls, recv_sem=lr,
-            device_id=(dom, lax.rem(rep + k, nrep)), device_id_type=MESH,
+            src_ref=ref, dst_ref=ref, send_sem=send_sem, recv_sem=recv_sem,
+            device_id=device, device_id_type=MESH,
         ).start()
+
+    for device in (right, left, across):
+        send_label(x, device, ls, lr)
+    send_label(x, sibling, ms, mr)
     share_own(0).start()
 
     def event(g):
@@ -171,21 +201,32 @@
             pltpu.make_async_copy(ref, ref, kr.at[way, g]).wait()
             share(way, g).start()
 
-        @pl.when(g + WINDOW < 12)
-        def _():
-            ring(0, g + WINDOW).start()
-            ring(1, g + WINDOW).start()
+        for way in range(2):
+            if g + WINDOW < 11:
+                ring(way, g + WINDOW).start()
+            elif g + WINDOW == 11:
+                last_ring(way, 0).start()
+                last_ring(way, 1).start()
+
+    def last_event(j):
+        for way in range(2):
+            ref = halves(way, c)[j]
+            pltpu.make_async_copy(ref, ref, ls_r.at[way, j]).wait()
+            last_share(way, j).start()
 
     log2e = math.log2(math.e) * (q_ref.shape[1] ** -0.5)
 
-    def unit(p, pieces):
+    def unit(p, pieces, cut=None):
         queries = inbox[p].reshape(half, -1)
         scores, onehots = [], []
         for _, xx, col, quarter in pieces:
-            at = pl.ds(pl.multiple_of(quarter * qrows, qrows), qrows)
+            size, start = qrows, quarter * qrows
+            if cut is not None:
+                size, start = hrows, start + cut * hrows
+            at = pl.ds(pl.multiple_of(start, size), size)
             keys = kbuf[p, xx * 2 + col, at, :]
             named = lab[xx * 2 + col, pl.ds(p, 1), at]
-            classes = lax.broadcasted_iota(jnp.int32, (NCLASS, qrows), 0)
+            classes = lax.broadcasted_iota(jnp.int32, (NCLASS, size), 0)
             onehots.append(jnp.where(classes == named, 1.0, 0.0).astype(jnp.bfloat16))
             scores.append(lax.dot_general(queries, keys, NT, preferred_element_type=jnp.float32))
         scores = jnp.concatenate(scores, axis=1)
@@ -206,7 +247,8 @@
     def own_unit(t, carry):
         p, i = lax.div(t, 2), lax.rem(t, 2)
         col = lax.rem(c + i, 2)
-        pl.when(t >= 2)(lambda: event(t + 1))
+        pl.when(t == 2)(lambda: event(3))
+        pl.when(t == 3)(lambda: event(4))
 
         @pl.when(i == 1)
         def _():
@@ -222,9 +264,8 @@
             pltpu.make_async_copy(ref, ref, bs_r.at[way, g]).wait()
 
     def ring_unit(g, carry):
-        pl.when(g == 1)(lambda: event(5))
-        pl.when(g == 4)(lambda: event(6))
-        pl.when(g >= 6)(lambda: event(g + 1))
+        for at, turn in ((1, 5), (4, 6), (6, 7), (7, 8), (8, 9), (9, 10)):
+            pl.when(g == at)(functools.partial(event, turn))
 
         @pl.when(g == 6)
         def _():
@@ -235,11 +276,25 @@
         unit(lax.div(g, 6), [landed(way, g, col) for col in (c, 1 - c) for way in range(2)])
         return carry
 
-    def last_unit(t, carry):
+    def late_unit(t, carry):
         g, i = 10 + lax.div(t, 2), lax.rem(t, 2)
-        pl.when(t == 1)(lambda: event(11))
-        pl.when(i == 1)(lambda: passed(g))
+
+        @pl.when(t == 1)
+        def _():
+            last_event(0)
+            passed(g)
+
+        pl.when(t == 2)(lambda: last_event(1))
         unit(PARTS - 1, [landed(way, g, lax.rem(c + i, 2)) for way in range(2)])
+        return carry
+
+    def last_unit(j, carry):
+        for way in range(2):
+            p, xx, col, quarter = landed(way, 11, 1 - c)
+            start = pl.multiple_of(quarter * qrows + j * hrows, hrows)
+            ref = kbuf.at[p, xx * 2 + col, pl.ds(start, hrows)]
+            pltpu.make_async_copy(ref, ref, lb_r.at[way, j]).wait()
+        unit(PARTS - 1, [landed(way, 11, 1 - c) for way in range(2)], j)
         return carry
 
     def finish(p):
@@ -255,21 +310,29 @@
         wire[p] = codes.reshape(nd, CAP, NCLASS)
 
     def send_back(p):
-        to_all(lambda d: wire.at[p, d], lambda d: ret.at[p, d], rs.at[p], rr.at[p])
-        to_all(lambda d: mout.at[p, d], lambda d: pin.at[p, d], ps.at[p], pr.at[p])
+        to_all(
+            (lambda d: mout.at[p, d], lambda d: pin.at[p, d], ps.at[p], pr.at[p]),
+            (lambda d: wire.at[p, d], lambda d: ret.at[p, d], rs.at[p], rr.at[p]),
+        )
 
     event(0)
+    far = pl.ds(0, nx - 1)
+    pltpu.make_async_copy(lab.at[far], lab.at[far], lr).wait()
+    for k in range(1, nx):
+        send_label(lax.rem(x + k, nx), sibling, ms, mr)
     event(1)
     share_own(1).start()
     m_s[...] = jnp.full(m_s.shape, -3.0e38, jnp.float32)
     acc[...] = jnp.zeros(acc.shape, jnp.float32)
     mask[...] = sel.T
-    pltpu.make_async_copy(lab.at[pl.ds(0, nrep - 1)], lab.at[pl.ds(0, nrep - 1)], lr).wait()
+    few = pl.ds(0, nx)
+    pltpu.make_async_copy(lab.at[few], lab.at[few], mr).wait()
     event(2)
     pltpu.make_async_copy(inbox, inbox, qr).wait()
     lax.fori_loop(0, 4, own_unit, 0)
     lax.fori_loop(0, 10, ring_unit, 0)
-    lax.fori_loop(0, 4, last_unit, 0)
+    lax.fori_loop(0, 3, late_unit, 0)
+    lax.fori_loop(0, 2, last_unit, 0)
     finish(1)
     send_back(1)
 
@@ -279,13 +342,17 @@
             share(way, g).wait_send()
         return carry
 
-    lax.fori_loop(0, 12, gone, 0)
+    lax.fori_loop(0, 11, gone, 0)
+    for way in range(2):
+        for j in range(2):
+            last_ring(way, j).wait_send()
+            last_share(way, j).wait_send()
     for p in range(PARTS):
         share_own(p).wait_send()
     others = pl.ds(0, nd - 1)
-    few = pl.ds(0, nrep - 1)
     pltpu.make_async_copy(outbox.at[:, others], outbox.at[:, others], qs).wait()
-    pltpu.make_async_copy(lab.at[few], lab.at[few], ls).wait()
+    pltpu.make_async_copy(lab.at[far], lab.at[far], ls).wait()
+    pltpu.make_async_copy(lab.at[few], lab.at[few], ms).wait()
 
     def left_home(p):
         pltpu.make_async_copy(wire.at[p, others], wire.at[p, others], rs.at[p]).wait()
@@ -358,11 +425,15 @@
             dma((PARTS,)),
             dma((PARTS,)),
             dma((PARTS,)),
-            dma((2, 12)),
-            dma((2, 12)),
-            dma((2, 12)),
-            dma((2, 12)),
-            dma, dma, dma, dma,
+            dma((2, 11)),
+            dma((2, 11)),
+            dma((2, 11)),
+            dma((2, 11)),
+            dma((2, 2)),
+            dma((2, 2)),
+            dma((2, 2)),
+            dma((2, 2)),
+            dma, dma, dma, dma, dma, dma,
             dma((PARTS,)),
             dma((PARTS,)),
             dma((PARTS,)),

time: 60.8 us -> 60.1 us (0.988)
    pallas_call x1, Pallas kernels: 59.2 us -> 58.6 us  [local(): pl.pallas_call(functools.partial(kernel, nd, nrep // 2), out_shape=jax.Sh...]
where the time goes in v4:
time: 60.1 us; the launch traced here: 59.9 us
  Pallas kernels  58.6 us (98%)
  local copies, waits for them, and re-layouts  1.38 us (2%)
    pallas_call x1, Pallas kernels, local(): pl.pallas_call(functools.partial(kernel, nd, nrep // 2), out_shape=jax.Sh...  58.6 us
    unnamed x1, local copies, waits for them, and re-layouts  1.38 us

profile of v4, /device:TPU:1, one launch (start us, length us, event | category | flops | bytes accessed | tf_op | source)
XLA Modules:
  0.0 59.9 jit_solution(3679396186394365396)
XLA Ops:
  0.0 58.6 %shard_map.46 = f32[64,128]{1,0:T(8,128)} custom-call(bf16[64,256]{1,0:T(8,128)(2,1)} %q_hbm.1, s32[8,64]{1,0:T(8,128)} %bitcast.1, bf16[2,1024,256]{2,1,0:T(8,128)(2,1)} %corpus_hbm.1, s32[2,1024]{1,0:T(2,128)} %labels_hbm.1), custom_call_target="tpu_custom_call" | custom-call | tf_op jit(solution)/shard_map/pallas_call | solution.py:405
  58.6 1.4 %copy.6 = f32[64,128]{1,0:T(8,128)} copy(f32[64,128]{1,0:T(8,128)} %shard_map.46) | data formatting | bytes 65536

commit v5 on v4

--- a/solution.py
+++ b/solution.py
@@ -264,13 +264,8 @@
             pltpu.make_async_copy(ref, ref, bs_r.at[way, g]).wait()
 
     def ring_unit(g, carry):
-        for at, turn in ((1, 5), (4, 6), (6, 7), (7, 8), (8, 9), (9, 10)):
+        for at, turn in ((0, 5), (3, 6), (5, 7), (7, 8), (8, 9), (9, 10)):
             pl.when(g == at)(functools.partial(event, turn))
-
-        @pl.when(g == 6)
-        def _():
-            finish(0)
-            send_back(0)
 
         passed(g)
         unit(lax.div(g, 6), [landed(way, g, col) for col in (c, 1 - c) for way in range(2)])
@@ -330,11 +325,20 @@
     event(2)
     pltpu.make_async_copy(inbox, inbox, qr).wait()
     lax.fori_loop(0, 4, own_unit, 0)
-    lax.fori_loop(0, 10, ring_unit, 0)
-    lax.fori_loop(0, 3, late_unit, 0)
-    lax.fori_loop(0, 2, last_unit, 0)
-    finish(1)
-    send_back(1)
+
+    def whole_part(p, carry):
+        lax.fori_loop(6 * p, 6 + 4 * p, ring_unit, 0)
+
+        @pl.when(p == 1)
+        def _():
+            lax.fori_loop(0, 3, late_unit, 0)
+            lax.fori_loop(0, 2, last_unit, 0)
+
+        finish(p)
+        send_back(p)
+        return carry
+
+    lax.fori_loop(0, PARTS, whole_part, 0)
 
     def gone(g, carry):
         for way in range(2):

time: 60.1 us -> 59.9 us (level)
  no operation moved by 1% of the time
where the time goes in v5:
time: 59.9 us; the launch traced here: 59.7 us
  Pallas kernels  58.3 us (97%)
  local copies, waits for them, and re-layouts  1.38 us (2%)
    pallas_call x1, Pallas kernels, local(): pl.pallas_call(functools.partial(kernel, nd, nrep // 2), out_shape=jax.Sh...  58.3 us
    unnamed x1, local copies, waits for them, and re-layouts  1.38 us

profile of v5, /device:TPU:1, one launch (start us, length us, event | category | flops | bytes accessed | tf_op | source)
XLA Modules:
  0.0 59.7 jit_solution(2907827999066167893)
XLA Ops:
  0.0 58.3 %shard_map.46 = f32[64,128]{1,0:T(8,128)} custom-call(bf16[64,256]{1,0:T(8,128)(2,1)} %q_hbm.1, s32[8,64]{1,0:T(8,128)} %bitcast.1, bf16[2,1024,256]{2,1,0:T(8,128)(2,1)} %corpus_hbm.1, s32[2,1024]{1,0:T(2,128)} %labels_hbm.1), custom_call_target="tpu_custom_call" | custom-call | tf_op jit(solution)/shard_map/pallas_call | solution.py:409
  58.4 1.4 %copy.6 = f32[64,128]{1,0:T(8,128)} copy(f32[64,128]{1,0:T(8,128)} %shard_map.46) | data formatting | bytes 65536

commit v6 on v5

--- a/solution.py
+++ b/solution.py
@@ -13,6 +13,8 @@
 PARTS = 2
 WINDOW = 4
 STEPS = 32767.0
+PEAK_UNIT = 2.0**-12
+MOST_UNIT = 2.0**-17
 MESH = pl.DeviceIdType.MESH
 NT = (((1,), (1,)), ((), ()))
 
@@ -45,8 +47,8 @@
 def kernel(
     nd, nx,
     q_hbm, probes_hbm, corpus_hbm, labels_hbm, out_ref,
-    q_ref, probes_ref, mask, outbox, inbox, kbuf, lab, acc, m_s, wire, mout, pin, ret,
-    fs, ko, so_s, so_r, ks, kr, bs_s, bs_r, ls_s, ls_r, lb_s, lb_r, qs, qr, ls, lr, ms, mr, rs, rr, ps, pr,
+    q_ref, probes_ref, mask, outbox, inbox, kbuf, lab, acc, m_s, wire, ret,
+    fs, ko, so_s, so_r, ks, kr, bs_s, bs_r, ls_s, ls_r, lb_s, lb_r, qs, qr, ls, lr, ms, mr, rs, rr,
 ):
     dom = lax.axis_index("dom")
     rep = lax.axis_index("rep")
@@ -296,17 +298,19 @@
         lane = lax.broadcasted_iota(jnp.int32, (half, 128), 1) % CAP
         slot = lax.broadcasted_iota(jnp.int32, (half, 128), 0) % CAP
         diag = jnp.where(lane == slot, m_s[p], 0.0).reshape(nd, CAP, 128)
-        mout[p, :, 0] = jnp.sum(diag, axis=1, keepdims=True)
+        peaks = jnp.sum(diag, axis=1, keepdims=True)
         sums = acc[p]
         most = jnp.max(sums, axis=1, keepdims=True)
-        diag = jnp.where(lane == slot, most, 0.0).reshape(nd, CAP, 128)
-        mout[p, :, 1] = jnp.sum(diag, axis=1, keepdims=True)
-        codes = jnp.round(sums * (STEPS / most)).astype(jnp.int32).astype(jnp.int16)
-        wire[p] = codes.reshape(nd, CAP, NCLASS)
+        most = (most * (1.0 / MOST_UNIT)).astype(jnp.int32) + 1
+        diag = jnp.where(lane == slot, most, 0).reshape(nd, CAP, 128)
+        wire[p, :, 8:9] = jnp.round(peaks * (1.0 / PEAK_UNIT)).astype(jnp.int32)
+        wire[p, :, 9:10] = jnp.sum(diag, axis=1, keepdims=True)
+        codes = jnp.round(sums * (STEPS / (most.astype(jnp.float32) * MOST_UNIT))).astype(jnp.int32)
+        codes = codes.reshape(nd, CAP, NCLASS)
+        wire[p, :, 0:8] = codes[:, :8] * 65536 + codes[:, 8:]
 
     def send_back(p):
         to_all(
-            (lambda d: mout.at[p, d], lambda d: pin.at[p, d], ps.at[p], pr.at[p]),
             (lambda d: wire.at[p, d], lambda d: ret.at[p, d], rs.at[p], rr.at[p]),
         )
 
@@ -360,7 +364,6 @@
 
     def left_home(p):
         pltpu.make_async_copy(wire.at[p, others], wire.at[p, others], rs.at[p]).wait()
-        pltpu.make_async_copy(mout.at[p, others], mout.at[p, others], ps.at[p]).wait()
 
     left_home(0)
 
@@ -370,15 +373,17 @@
     top = jnp.full((nq, 1), -3.0e38, jnp.float32)
     total = jnp.zeros((nq, NCLASS), jnp.float32)
     for p in range(PARTS):
-        pltpu.make_async_copy(pin.at[p], pin.at[p], pr.at[p]).wait()
+        pltpu.make_async_copy(ret.at[p], ret.at[p], rr.at[p]).wait()
         found = []
         new_top = top
         for g in range(half // 128):
-            line = jnp.zeros((1, 128), jnp.float32)
-            most = jnp.zeros((1, 128), jnp.float32)
+            line = jnp.zeros((1, 128), jnp.int32)
+            most = jnp.zeros((1, 128), jnp.int32)
             for i in range(per):
-                line = jnp.where(lane == i, pin[p, g * per + i, 0], line)
-                most = jnp.where(lane == i, pin[p, g * per + i, 1], most)
+                line = jnp.where(lane == i, ret[p, g * per + i, 8:9], line)
+                most = jnp.where(lane == i, ret[p, g * per + i, 9:10], most)
+            line = line.astype(jnp.float32) * PEAK_UNIT
+            most = most.astype(jnp.float32) * MOST_UNIT
             chosen = mask[:, p * half + g * 128 : p * half + (g + 1) * 128] > 0.0
             found.append((chosen, line, most))
             best = jnp.max(jnp.where(chosen, line, -3.0e38), axis=1, keepdims=True)
@@ -389,8 +394,9 @@
             jnp.where(chosen, jnp.exp2(jnp.where(chosen, line - top, 0.0) * log2e) * (most / STEPS), 0.0)
             for chosen, line, most in found
         ]
-        pltpu.make_async_copy(ret.at[p], ret.at[p], rr.at[p]).wait()
-        codes = ret[p].astype(jnp.int32).astype(jnp.float32).reshape(half, NCLASS)
+        pairs = ret[p, :, 0:8]
+        codes = jnp.concatenate([lax.shift_right_logical(pairs, 16), pairs & 65535], axis=1)
+        codes = codes.astype(jnp.float32).reshape(half, NCLASS)
         total += jnp.dot(
             jnp.concatenate(factors, axis=1), codes,
             precision=lax.Precision.HIGHEST, preferred_element_type=jnp.float32,
@@ -421,10 +427,8 @@
             pltpu.VMEM((nrep, PARTS, rows), jnp.int32),
             pltpu.VMEM((PARTS, half, NCLASS), jnp.float32),
             pltpu.VMEM((PARTS, half, 128), jnp.float32),
-            pltpu.VMEM((PARTS, nd, CAP, NCLASS), jnp.int16),
-            pltpu.VMEM((PARTS, nd, 2, 1, 128), jnp.float32),
-            pltpu.VMEM((PARTS, nd, 2, 1, 128), jnp.float32),
-            pltpu.VMEM((PARTS, nd, CAP, NCLASS), jnp.int16),
+            pltpu.VMEM((PARTS, nd, 10, NCLASS), jnp.int32),
+            pltpu.VMEM((PARTS, nd, 10, NCLASS), jnp.int32),
             dma((3,)),
             dma((PARTS,)),
             dma((PARTS,)),
@@ -440,8 +444,6 @@
             dma, dma, dma, dma, dma, dma,
             dma((PARTS,)),
             dma((PARTS,)),
-            dma((PARTS,)),
-            dma((PARTS,)),
         ],
         compiler_params=pltpu.CompilerParams(
             collective_id=0, has_side_effects=True, vmem_limit_bytes=62 * 1024 * 1024

time: 59.9 us -> 59.9 us (level)
  no operation moved by 1% of the time
where the time goes in v6:
time: 59.9 us; the launch traced here: 59.7 us
  Pallas kernels  58.4 us (97%)
  local copies, waits for them, and re-layouts  1.38 us (2%)
    pallas_call x1, Pallas kernels, local(): pl.pallas_call(functools.partial(kernel, nd, nrep // 2), out_shape=jax.Sh...  58.4 us
    unnamed x1, local copies, waits for them, and re-layouts  1.38 us

profile of v6, /device:TPU:1, one launch (start us, length us, event | category | flops | bytes accessed | tf_op | source)
XLA Modules:
  0.0 59.7 jit_solution(3385078458298215053)
XLA Ops:
  0.0 58.4 %shard_map.46 = f32[64,128]{1,0:T(8,128)} custom-call(bf16[64,256]{1,0:T(8,128)(2,1)} %q_hbm.1, s32[8,64]{1,0:T(8,128)} %bitcast.1, bf16[2,1024,256]{2,1,0:T(8,128)(2,1)} %corpus_hbm.1, s32[2,1024]{1,0:T(2,128)} %labels_hbm.1), custom_call_target="tpu_custom_call" | custom-call | tf_op jit(solution)/shard_map/pallas_call | solution.py:415
  58.4 1.4 %copy.6 = f32[64,128]{1,0:T(8,128)} copy(f32[64,128]{1,0:T(8,128)} %shard_map.46) | data formatting | bytes 65536
